TPU v7x, 128 devices: a whole 4x4x4 slice. The times are simulated.
128 devices in a mesh: group: 4 (over y), dev: 32 (over z, x, core).
Axes of the slice: x: 4, y: 4, z: 4, core: 2. Of those that a mesh axis runs over, the one named last changes fastest.
Arguments:
- source_points: bfloat16 [262144, 128], P(('group', 'dev')), may hold values from -20 to 20
- target_points: bfloat16 [262144, 128], P(('group', 'dev')), may hold values from -20 to 20
- source_logw: float32 [262144], P(('group', 'dev')), may hold values from -1 to 1
- target_logw: float32 [262144], P(('group', 'dev')), may hold values from -1 to 1
- pair_targets: int32 [512, 8], replicated, may hold values from 0 to 511, as said below
- pair_count: int32 [512], replicated, may hold values from 2 to 8, as said below
Outputs:
- source_potential: float32 [262144], P(('group', 'dev'))
- target_potential: float32 [262144], P(('group', 'dev'))
- mapped_points: float32 [262144, 128], P(('group', 'dev'))
Inputs may be any that keep to these rules, and one draw needn't show every extreme that they name: `pair_targets`: slot 0 of row b names target block b. The names in the slots of one row are distinct. Target block t belongs to device t // 4 in the order of group then dev. Among all slots of the 4 rows of one device, the blocks named that belong to one other device are all the same block. A name outside the row's own group stands only in slot 1 and belongs to the device with the same index along dev. `pair_count`: some row uses all 8 slots.
All inputs are finite; a program needn't handle non-finite values.
Results may differ from a plain program's by a relative error of at most 0.0025.
Values may be sent and summed in bfloat16 or wider, within the bound.
A program may use at most 64 MiB of HBM per device.

v0:
```python
import math

import jax
import jax.numpy as jnp
from jax import lax
from jax.sharding import PartitionSpec as P

BLOCK = 512
EMB = 128
BLK_DEV = 4
SLOTS = 8


NEG_FILL = -1e30


def block_scores(left, right, factor):
    return (
        lax.dot_general(left, right, (((1,), (1,)), ((), ())), preferred_element_type=jnp.float32)
        * factor
    )


def outgoing(blocks, wanted, picked):
    chosen = jnp.take(blocks, picked, axis=0)
    shape = (wanted.shape[0],) + (1,) * (chosen.ndim - 1)
    return jnp.where(wanted.reshape(shape), chosen, jnp.zeros_like(chosen))


def requests(targets, counts, owner_self, skipped, blk_count):
    slot_count = targets.shape[2]
    active = jnp.arange(slot_count, dtype=jnp.int32)[None, None, :] < counts[:, :, None]
    match = active & (targets // blk_count == owner_self) & jnp.logical_not(skipped)[:, None, None]
    wanted = jnp.any(match, axis=(1, 2))
    picked = jnp.max(jnp.where(match, targets % blk_count, 0), axis=(1, 2))
    return (wanted, picked)


def select(tables, position, blk_count, dev_count):
    local_tab, dev_tab, group_tab = tables
    from_local = local_tab[jnp.clip(position, 0, blk_count - 1)]
    from_dev = dev_tab[jnp.clip(position - blk_count, 0, dev_count - 1)]
    from_group = group_tab[jnp.clip(position - blk_count - dev_count, 0, group_tab.shape[0] - 1)]
    return jnp.where(
        position < blk_count,
        from_local,
        jnp.where(position < blk_count + dev_count, from_dev, from_group),
    )


def shards(source_points, target_points, source_logw, target_logw, pair_targets, pair_count):
    group_count = lax.axis_size("group")
    dev_count = lax.axis_size("dev")
    group_idx = lax.axis_index("group")
    dev_idx = lax.axis_index("dev")
    myself = group_idx * dev_count + dev_idx
    blk_count = BLK_DEV
    blk_rows = BLOCK
    slot_count = SLOTS
    factor = 1.0 / math.sqrt(EMB)
    sources = source_points.reshape(blk_count, blk_rows, EMB)
    targets_loc = target_points.reshape(blk_count, blk_rows, EMB)
    log_src = source_logw.reshape(blk_count, blk_rows)
    log_tgt = target_logw.reshape(blk_count, blk_rows)
    own_targets = lax.dynamic_slice_in_dim(pair_targets, myself * blk_count, blk_count, 0)
    own_counts = lax.dynamic_slice_in_dim(pair_count, myself * blk_count, blk_count, 0)
    active = jnp.arange(slot_count, dtype=jnp.int32)[None, :] < own_counts[:, None]
    owners = own_targets // blk_count
    table_pos = jnp.where(
        owners == myself,
        own_targets % blk_count,
        jnp.where(
            owners // dev_count == group_idx,
            blk_count + owners % dev_count,
            blk_count + dev_count + owners // dev_count,
        ),
    )
    ntable = blk_count + dev_count + group_count
    everything = pair_targets.reshape(group_count, dev_count, blk_count, slot_count)
    counts_all = pair_count.reshape(group_count, dev_count, blk_count)
    group_targets = lax.dynamic_index_in_dim(everything, group_idx, 0, keepdims=False)
    group_counts = lax.dynamic_index_in_dim(counts_all, group_idx, 0, keepdims=False)
    peer_ids = jnp.arange(dev_count, dtype=jnp.int32)
    want_dev, pick_dev = requests(
        group_targets, group_counts, myself, peer_ids == dev_idx, blk_count
    )
    lane_targets = lax.dynamic_index_in_dim(everything, dev_idx, 1, keepdims=False)
    lane_counts = lax.dynamic_index_in_dim(counts_all, dev_idx, 1, keepdims=False)
    group_ids = jnp.arange(group_count, dtype=jnp.int32)
    want_grp, pick_grp = requests(
        lane_targets, lane_counts, myself, group_ids == group_idx, blk_count
    )
    dev_rows = lax.all_to_all(
        outgoing(targets_loc, want_dev, pick_dev), "dev", split_axis=0, concat_axis=0, tiled=True
    )
    lookup = (
        targets_loc,
        dev_rows,
        lax.all_to_all(
            outgoing(targets_loc, want_grp, pick_grp),
            "group",
            split_axis=0,
            concat_axis=0,
            tiled=True,
        ),
    )
    pair_ids = jnp.arange(blk_count * slot_count, dtype=jnp.int32)

    def row_pass(dual_tab):

        def row_advance(carry_in, pair_id):
            blk_id = pair_id // slot_count
            slot_id = pair_id % slot_count

            def row_include(state_in):
                row_high, row_sum = state_in
                position = table_pos[blk_id, slot_id]
                scores = block_scores(
                    sources[blk_id], select(lookup, position, blk_count, dev_count), factor
                )
                scores = scores + select(dual_tab, position, blk_count, dev_count)[None, :]
                old_high = row_high[blk_id]
                new_high = jnp.maximum(old_high, jnp.max(scores, axis=1))
                new_sum = row_sum[blk_id] * jnp.exp(old_high - new_high) + jnp.sum(
                    jnp.exp(scores - new_high[:, None]), axis=1
                )
                return (row_high.at[blk_id].set(new_high), row_sum.at[blk_id].set(new_sum))

            return (
                lax.cond(
                    active[blk_id, slot_id], row_include, lambda unchanged: unchanged, carry_in
                ),
                None,
            )

        start_state = (
            jnp.full((blk_count, blk_rows), NEG_FILL, jnp.float32),
            jnp.zeros((blk_count, blk_rows), jnp.float32),
        )
        (row_high, row_sum), _ = lax.scan(row_advance, start_state, pair_ids)
        return row_high + jnp.log(row_sum)

    def column_pass(potential, dual_tab, row_lse, mapped):

        def column_advance(carry_in, pair_id):
            blk_id = pair_id // slot_count
            slot_id = pair_id % slot_count

            def column_include(state_in):
                col_max, col_sum, numerator, denominator = state_in
                position = table_pos[blk_id, slot_id]
                rows_y = select(lookup, position, blk_count, dev_count)
                scores = block_scores(sources[blk_id], rows_y, factor)
                shifted = scores + potential[blk_id][:, None]
                part_max = jnp.max(shifted, axis=0)
                part_sum = jnp.sum(jnp.exp(shifted - part_max[None, :]), axis=0)
                old_max = col_max[position]
                new_max = jnp.maximum(old_max, part_max)
                new_sum = col_sum[position] * jnp.exp(old_max - new_max) + part_sum * jnp.exp(
                    part_max - new_max
                )
                col_max = col_max.at[position].set(new_max)
                col_sum = col_sum.at[position].set(new_sum)
                if mapped:
                    plan = jnp.exp(
                        scores
                        + select(dual_tab, position, blk_count, dev_count)[None, :]
                        - row_lse[blk_id][:, None]
                    )
                    numerator = numerator.at[blk_id].add(
                        jnp.dot(
                            plan.astype(jnp.bfloat16), rows_y, preferred_element_type=jnp.float32
                        )
                    )
                    denominator = denominator.at[blk_id].add(jnp.sum(plan, axis=1))
                return (col_max, col_sum, numerator, denominator)

            return (
                lax.cond(
                    active[blk_id, slot_id], column_include, lambda unchanged: unchanged, carry_in
                ),
                None,
            )

        start_state = (
            jnp.full((ntable, blk_rows), NEG_FILL, jnp.float32),
            jnp.zeros((ntable, blk_rows), jnp.float32),
            jnp.zeros((blk_count, blk_rows, EMB), jnp.float32),
            jnp.zeros((blk_count, blk_rows), jnp.float32),
        )
        result, _ = lax.scan(column_advance, start_state, pair_ids)
        return result

    wanted_all = jnp.concatenate([want_dev, want_grp], axis=0)
    picked_all = jnp.concatenate([pick_dev, pick_grp], axis=0)
    chosen = wanted_all[:, None] & (
        picked_all[:, None] == jnp.arange(blk_count, dtype=jnp.int32)[None, :]
    )
    chosen3 = chosen[:, :, None]
    mid = blk_count + dev_count

    def settle(col_max, col_sum):
        dev_max, dev_sum = (
            lax.all_to_all(col_max[blk_count:mid], "dev", split_axis=0, concat_axis=0, tiled=True),
            lax.all_to_all(col_sum[blk_count:mid], "dev", split_axis=0, concat_axis=0, tiled=True),
        )
        grp_max, grp_sum = (
            lax.all_to_all(col_max[mid:], "group", split_axis=0, concat_axis=0, tiled=True),
            lax.all_to_all(col_sum[mid:], "group", split_axis=0, concat_axis=0, tiled=True),
        )
        in_max = jnp.concatenate([dev_max, grp_max], axis=0)[:, None, :]
        in_sum = jnp.concatenate([dev_sum, grp_sum], axis=0)[:, None, :]
        masked_max = jnp.where(chosen3, in_max, NEG_FILL)
        highest = jnp.maximum(col_max[:blk_count], jnp.max(masked_max, axis=0))
        summed = col_sum[:blk_count] * jnp.exp(col_max[:blk_count] - highest)
        summed = summed + jnp.sum(
            jnp.where(chosen3, in_sum * jnp.exp(masked_max - highest[None]), 0.0), axis=0
        )
        return log_tgt - (highest + jnp.log(summed))

    zero_duals = (
        jnp.zeros((blk_count, blk_rows), jnp.float32),
        jnp.zeros((dev_count, blk_rows), jnp.float32),
        jnp.zeros((group_count, blk_rows), jnp.float32),
    )
    row_lse1 = row_pass(zero_duals)
    first_source = log_src - row_lse1
    col_max, col_sum, unused_num, unused_den = column_pass(
        first_source, zero_duals, row_lse1, False
    )
    first_target = settle(col_max, col_sum)
    dual_tab = (
        first_target,
        lax.all_to_all(
            outgoing(first_target, want_dev, pick_dev),
            "dev",
            split_axis=0,
            concat_axis=0,
            tiled=True,
        ),
        lax.all_to_all(
            outgoing(first_target, want_grp, pick_grp),
            "group",
            split_axis=0,
            concat_axis=0,
            tiled=True,
        ),
    )
    row_lse2 = row_pass(dual_tab)
    source_potential = log_src - row_lse2
    col_max, col_sum, numerator, denominator = column_pass(
        source_potential, dual_tab, row_lse2, True
    )
    target_potential = settle(col_max, col_sum)
    mapped_points = numerator / denominator[:, :, None]
    return (
        source_potential.reshape(blk_count * blk_rows),
        target_potential.reshape(blk_count * blk_rows),
        mapped_points.reshape(blk_count * blk_rows, EMB),
    )


def solution(mesh):
    return jax.shard_map(
        shards,
        mesh=mesh,
        in_specs=(
            P(("group", "dev"), None),
            P(("group", "dev"), None),
            P(("group", "dev")),
            P(("group", "dev")),
            P(),
            P(),
        ),
        out_specs=(P(("group", "dev")), P(("group", "dev")), P(("group", "dev"), None)),
        check_vma=False,
    )
```

profile of v0, /device:TPU:1, one launch (start us, length us, event | category | flops | bytes accessed | tf_op | source)
XLA Modules:
  0.0 1964.0 jit_solution(15773122852838894691)
XLA Ops:
  5.5 5.0 all-to-all-start.1
  19.7 9.2 all-to-all-start
  29.8 49.4 %all-to-all-done = bf16[32,512,128]{2,1,0:T(8,128)(2,1)} async-done(((bf16[32,512,128]{2,1,0:T(8,128)(2,1)}), bf16[32,512,128]{2,1,0:T(8,128)(2,1)}, u32[]{:S(2)}, u32[]{:S(2)}) %all-to-all-start) | async-done | bytes 4194336 | tf_op jit(solution)/shard_map/all_to_all | solution.py:93
  79.2 237.8 %while.70 = (s32[]{:T(128)}, f32[4,512]{1,0:T(4,128)S(1)}, f32[4,512]{1,0:T(4,128)S(1)}, s32[32]{0:T(128)S(1)}, pred[4,8]{1,0:T(4,128)(4,1)S(1)}, /*index=5*/bf1...) while((s32[]{:T(128)}, f32[4,512]{1,0:T(4,128)S(1)}, ...), condition=%wide.region_10.11_spmd, body=%wide.region_4.10_spmd.sunk | while | flops 68291632 | bytes 2664200 | solution.py:140
  83.8 7.5 conditional.8
  95.9 7.5 conditional.8
  108.0 7.5 conditional.8
  143.2 7.5 conditional.8
  155.3 7.5 conditional.8
  167.5 7.5 conditional.8
  202.7 7.5 conditional.8
  214.8 7.5 conditional.8
  226.9 7.5 conditional.8
  262.1 7.5 conditional.8
  274.2 7.5 conditional.8
  286.4 7.5 conditional.8
  317.0 263.4 %while.71 = (s32[]{:T(128)}, f32[40,512]{1,0:T(8,128)S(1)}, f32[40,512]{1,0:T(8,128)S(1)}, s32[32]{0:T(128)S(1)}, pred[4,8]{1,0:T(4,128)(4,1)S(1)}, /*index=5*/s...) while((s32[]{:T(128)}, f32[40,512]{1,0:T(8,128)S(1)}, ...), condition=%wide.region_17.18_spmd, body=%wide.region_11.17_spmd.sunk | while | flops 68553784 | bytes 2655051 | solution.py:191
  321.5 10.0 conditional.9
  336.0 10.0 conditional.9
  350.5 10.0 conditional.9
  387.4 10.0 conditional.9
  401.8 10.0 conditional.9
  416.3 10.0 conditional.9
  453.2 10.0 conditional.9
  467.7 10.0 conditional.9
  482.2 10.0 conditional.9
  519.1 10.0 conditional.9
  533.5 10.0 conditional.9
  548.0 10.0 conditional.9
  581.1 354.9 %all-to-all-start.5 = ((f32[4,1,512]{2,1,0:T(1,128)}), f32[4,1,512]{2,1,0:T(1,128)S(1)}, u32[]{:S(2)}, u32[]{:S(2)}) async-start(f32[4,1,512]{2,1,0:T(1,128)} %all_to_all.93), calls=%async_computation.5 | async-start | bytes 16384 | tf_op jit(solution)/shard_map/all_to_all | solution.py:209
  947.5 8.5 all-to-all-start.2
  956.8 6.5 all-to-all-done.2
  967.5 7.2 all-to-all-done.4
  984.2 5.1 all-to-all-start.6
  989.3 7.4 all-to-all-done.6
  996.8 238.2 %while.72 = (s32[]{:T(128)}, f32[4,512]{1,0:T(4,128)S(1)}, f32[4,512]{1,0:T(4,128)S(1)}, s32[32]{0:T(128)S(1)}, pred[4,8]{1,0:T(4,128)(4,1)S(1)}, /*index=5*/bf1...) while((s32[]{:T(128)}, f32[4,512]{1,0:T(4,128)S(1)}, ...), condition=%wide.region_26.27_spmd, body=%wide.region_20.26_spmd.sunk | while | flops 68554800 | bytes 2674502 | solution.py:140
  1001.3 7.6 conditional.10
  1013.5 7.6 conditional.10
  1025.7 7.6 conditional.10
  1060.9 7.6 conditional.10
  1073.1 7.6 conditional.10
  1085.2 7.6 conditional.10
  1120.4 7.6 conditional.10
  1132.6 7.6 conditional.10
  1144.8 7.6 conditional.10
  1180.0 7.6 conditional.10
  1192.2 7.6 conditional.10
  1204.3 7.6 conditional.10
  1235.1 291.0 %while.73 = (s32[]{:T(128)}, f32[40,512]{1,0:T(8,128)S(1)}, f32[40,512]{1,0:T(8,128)S(1)}, f32[4,512,128]{2,1,0:T(8,128)S(1)}, f32[4,512]{1,0:T(4,128)S(1)}, /*i...) while((s32[]{:T(128)}, f32[40,512]{1,0:T(8,128)S(1)}, ...), condition=%wide.region_36.37_spmd, body=%wide.region_27.36_spmd.sunk | while | flops 137630304 | bytes 4656265 | solution.py:191
  1239.6 12.3 conditional.11
  1256.3 12.3 conditional.11
  1273.1 12.3 conditional.11
  1312.3 12.3 conditional.11
  1329.1 12.3 conditional.11
  1345.9 12.3 conditional.11
  1385.1 12.3 conditional.11
  1401.8 12.3 conditional.11
  1418.6 12.3 conditional.11
  1457.8 12.3 conditional.11
  1474.6 12.3 conditional.11
  1491.4 12.3 conditional.11
  1526.7 399.1 %all-to-all-start.11 = ((f32[4,1,512]{2,1,0:T(1,128)}), f32[4,1,512]{2,1,0:T(1,128)S(1)}, u32[]{:S(2)}, u32[]{:S(2)}) async-start(f32[4,1,512]{2,1,0:T(1,128)} %all_to_all.109), calls=%async_computation.11 | async-start | bytes 16384 | tf_op jit(solution)/shard_map/all_to_all | solution.py:209
  1937.4 7.1 all-to-all-start.8
  1955.9 7.2 all-to-all-done.10
  (999 shorter events, 480.2 us)
Async XLA Ops:
  0.6 11.3 copy-start
  5.5 14.3 all-to-all-start.1
  19.7 10.0 copy-start.4
  19.7 59.5 %copy-start.1 = (bf16[2048,128]{1,0:T(8,128)(2,1)S(1)}, bf16[2048,128]{1,0:T(8,128)(2,1)}, u32[]{:S(2)}) copy-start(bf16[2048,128]{1,0:T(8,128)(2,1)} %param.42) | copy-start | bytes 1572868
  19.7 59.4 %all-to-all-start = ((bf16[32,512,128]{2,1,0:T(8,128)(2,1)}), bf16[32,512,128]{2,1,0:T(8,128)(2,1)}, u32[]{:S(2)}, u32[]{:S(2)}) async-start(bf16[32,512,128]{2,1,0:T(8,128)(2,1)} %select_select_fusion.1), calls=%async_computation | async-start | bytes 8388608 | tf_op jit(solution)/shard_map/all_to_all | solution.py:93
  317.0 639.1 %copy-start.5 = (f32[2048]{0:T(1024)S(1)}, f32[2048]{0:T(1024)}, u32[]{:S(2)}) copy-start(f32[2048]{0:T(1024)} %param.45) | copy-start | bytes 24580
  581.1 359.1 %all-to-all-start.5 = ((f32[4,1,512]{2,1,0:T(1,128)}), f32[4,1,512]{2,1,0:T(1,128)S(1)}, u32[]{:S(2)}, u32[]{:S(2)}) async-start(f32[4,1,512]{2,1,0:T(1,128)} %all_to_all.93), calls=%async_computation.5 | async-start | bytes 16384 | tf_op jit(solution)/shard_map/all_to_all | solution.py:209
  940.1 7.4 all-to-all-start.3
  947.5 15.8 all-to-all-start.2
  963.4 11.3 all-to-all-start.4
  976.8 7.4 all-to-all-start.7
  984.2 12.5 all-to-all-start.6
  1239.6 9.5 copy-start.3
  1239.6 10.2 copy-start.2
  1256.4 9.5 copy-start.3
  1256.4 10.2 copy-start.2
  1273.1 9.5 copy-start.3
  1273.1 10.2 copy-start.2
  1312.3 9.5 copy-start.3
  1312.3 10.2 copy-start.2
  1329.1 9.5 copy-start.3
  1329.1 10.2 copy-start.2
  1345.9 9.5 copy-start.3
  1345.9 10.2 copy-start.2
  1385.1 9.5 copy-start.3
  1385.1 10.2 copy-start.2
  1401.9 9.5 copy-start.3
  1401.9 10.2 copy-start.2
  1418.6 9.5 copy-start.3
  1418.7 10.2 copy-start.2
  1457.8 9.5 copy-start.3
  1457.8 10.2 copy-start.2
  1474.6 9.5 copy-start.3
  1474.6 10.2 copy-start.2
  1491.4 9.5 copy-start.3
  1491.4 10.2 copy-start.2
  1526.7 403.2 %all-to-all-start.11 = ((f32[4,1,512]{2,1,0:T(1,128)}), f32[4,1,512]{2,1,0:T(1,128)S(1)}, u32[]{:S(2)}, u32[]{:S(2)}) async-start(f32[4,1,512]{2,1,0:T(1,128)} %all_to_all.109), calls=%async_computation.11 | async-start | bytes 16384 | tf_op jit(solution)/shard_map/all_to_all | solution.py:209
  1930.0 7.4 all-to-all-start.9
  1937.4 14.4 all-to-all-start.8
  1951.8 11.3 all-to-all-start.10
where the time goes:
time: 1980 us; the launch traced here: 1960 us
  starting transfers between devices  806 us (41%)
  loops' own time  617 us (31%)
  local copies, waits for them, and re-layouts  209 us (11%)
  other arithmetic  169 us (9%)
  waiting for transfers between devices  99.8 us (5%)
  matrix products  61 us (3%)
    all_to_all x2, starting transfers between devices, settle(): lax.all_to_all(col_sum[mid:], 'group', split_axis=0, concat_axis=0, tiled...  754 us
    another operation x2, loops' own time, row_pass(): (row_high, row_sum), _ = lax.scan(row_advance, start_state, pair_ids)  214 us
    another operation x2, loops' own time, column_pass(): result, _ = lax.scan(column_advance, start_state, pair_ids)  209 us
    another operation x144, other arithmetic  134 us
    another operation x64, loops' own time, column_advance(): lax.cond(active[blk_id, slot_id], column_include, lambda unchanged: uncha...  124 us
    dynamic_slice x128, local copies, waits for them, and re-layouts, row_pass(): (row_high, row_sum), _ = lax.scan(row_advance, start_state, pair_ids)  75 us
    another operation x64, loops' own time, row_advance(): lax.cond(active[blk_id, slot_id], row_include, lambda unchanged: unchange...  70.6 us
    all_to_all x1, waiting for transfers between devices, shards(): lax.all_to_all(outgoing(targets_loc, want_dev, pick_dev), 'dev', split_ax...  49.4 us
  transfers between devices with their start and end apart: 12, of which 11 were waited for; matrix products, arithmetic and copies ran while one was open for 1% of the time, Pallas kernels for 0%

commit v1 on v0

v1 whole, which is shorter than its diff:
```python
import functools
import math

import jax
import jax.numpy as jnp
from jax import lax
from jax.experimental import pallas as pl
from jax.experimental.pallas import tpu as pltpu
from jax.sharding import PartitionSpec as P

BLOCK = 512
EMB = 128
BLK_DEV = 4
SLOTS = 8
LANES = 128
NEG_FILL = -1e30
LOG2E = math.log2(math.e)
ROW_LOW, ROW_HIGH, COL_LOW = 1e-6, 1e30, 1e-22
MESH = pl.DeviceIdType.MESH
VMEM_LIMIT = 48 * 2**20


def requests(targets, counts, owner_self, skipped, blk_count):
    slot_count = targets.shape[2]
    active = jnp.arange(slot_count, dtype=jnp.int32)[None, None, :] < counts[:, :, None]
    match = active & (targets // blk_count == owner_self) & jnp.logical_not(skipped)[:, None, None]
    return jnp.max(jnp.where(match, targets % blk_count, -1), axis=(1, 2))


def raw_scores(left, right):
    return lax.dot_general(left, right, (((1,), (1,)), ((), ())), preferred_element_type=jnp.float32)


def as_columns(row):
    return jnp.transpose(jnp.broadcast_to(row, (LANES, row.shape[1])))


def as_row(columns):
    return jnp.transpose(columns)[0:1]


def weight_rows(weights):
    high = weights.astype(jnp.bfloat16).astype(jnp.float32)
    rest = weights - high
    middle = rest.astype(jnp.bfloat16).astype(jnp.float32)
    low = rest - middle
    at = lax.broadcasted_iota(jnp.int32, (16, weights.shape[1]), 0)
    zero = jnp.zeros((16, weights.shape[1]), jnp.float32)
    rows = jnp.where(at == 0, high, jnp.where(at == 1, middle, jnp.where(at == 2, low, zero)))
    return rows.astype(jnp.bfloat16)


def fetch_all(pos_ref, cnt_ref, loc_ref, dev_ref, grp_ref, held, sems):
    blocks, slots = BLK_DEV, SLOTS
    dev_count = dev_ref.shape[0]

    @pl.loop(0, blocks * slots)
    def _(at):
        position = pos_ref[at]
        active = lax.rem(at, slots) < cnt_ref[at // slots]

        @pl.when(active & (position < blocks))
        def _():
            pltpu.make_async_copy(loc_ref.at[position], held.at[at], sems.at[at]).start()

        @pl.when(active & (position >= blocks) & (position < blocks + dev_count))
        def _():
            pltpu.make_async_copy(dev_ref.at[position - blocks], held.at[at], sems.at[at]).start()

        @pl.when(active & (position >= blocks + dev_count))
        def _():
            pltpu.make_async_copy(
                grp_ref.at[position - blocks - dev_count], held.at[at], sems.at[at]
            ).start()


def first_kernel(
    pos_ref, cnt_ref, src_ref, logw_ref, loc_ref, dev_ref, grp_ref,
    fs_ref, part_ref,
    held, kept, row_acc, col_max, col_sum, tab_max, tab_sum, col_tmp, sems,
):
    factor = 1.0 / math.sqrt(EMB)
    scale = factor * LOG2E
    rows = src_ref.shape[1]
    fetch_all(pos_ref, cnt_ref, loc_ref, dev_ref, grp_ref, held, sems)
    tab_max[...] = jnp.full_like(tab_max, NEG_FILL)
    tab_sum[...] = jnp.zeros_like(tab_sum)

    @pl.loop(0, BLK_DEV)
    def _(blk):
        count = cnt_ref[blk]
        row_acc[...] = jnp.zeros_like(row_acc)
        col_max[...] = jnp.zeros_like(col_max)
        col_sum[...] = jnp.ones_like(col_sum)

        @pl.loop(0, count)
        def _(slot):
            at = blk * SLOTS + slot
            pltpu.make_async_copy(loc_ref.at[0], held.at[at], sems.at[at]).wait()
            for part in range(rows // LANES):
                span = pl.ds(part * LANES, LANES)
                kern = jnp.exp2(raw_scores(src_ref[blk, span, :], held[at]) * scale)
                total = kern[:, :LANES]
                for lane in range(1, rows // LANES):
                    total = total + kern[:, lane * LANES : (lane + 1) * LANES]
                row_acc[span, :] += total
                kept[slot, span, :] = kern.astype(jnp.bfloat16)

        row_sum = lax.dot_general(
            jnp.ones((8, LANES), jnp.float32),
            row_acc[...],
            (((1,), (1,)), ((), ())),
            precision=lax.Precision.HIGHEST,
            preferred_element_type=jnp.float32,
        )[0:1]
        logw = logw_ref[blk]
        fs_ref[blk] = logw - jnp.log(row_sum)
        weights = weight_rows(jnp.exp(logw) / row_sum)

        @pl.loop(0, count)
        def _(slot):
            col_sum[slot] = jnp.sum(
                jnp.dot(weights, kept[slot], preferred_element_type=jnp.float32),
                axis=0,
                keepdims=True,
            )

        row_fine = (row_sum >= ROW_LOW) & (row_sum <= ROW_HIGH)
        fine = jnp.min(jnp.where(row_fine, 1.0, 0.0))
        col_fine = jnp.where(col_sum[...] >= COL_LOW, 1.0, 0.0)
        fine = jnp.minimum(fine, jnp.min(jnp.min(col_fine, axis=0)))

        @pl.when(fine < 0.5)
        def _():
            row_acc[...] = jnp.full_like(row_acc, NEG_FILL)
            col_tmp[...] = jnp.zeros_like(col_tmp)

            @pl.loop(0, count)
            def _(slot):
                at = blk * SLOTS + slot
                for part in range(rows // LANES):
                    span = pl.ds(part * LANES, LANES)
                    scores = raw_scores(src_ref[blk, span, :], held[at]) * factor
                    old = row_acc[span, :]
                    new = jnp.maximum(old, jnp.max(scores, axis=1, keepdims=True))
                    here = jnp.sum(jnp.exp(scores - new[:, 0:1]), axis=1, keepdims=True)
                    col_tmp[span, :] = col_tmp[span, :] * jnp.exp(old - new) + here
                    row_acc[span, :] = new

            source = as_columns(logw_ref[blk]) - (row_acc[...] + jnp.log(col_tmp[...]))
            row_acc[...] = source
            fs_ref[blk] = as_row(source)

            @pl.loop(0, count)
            def _(slot):
                at = blk * SLOTS + slot
                high = jnp.full((1, rows), NEG_FILL, jnp.float32)
                total = jnp.zeros((1, rows), jnp.float32)
                for part in range(rows // LANES):
                    span = pl.ds(part * LANES, LANES)
                    scores = raw_scores(src_ref[blk, span, :], held[at]) * factor
                    scores = scores + row_acc[span, 0:1]
                    new = jnp.maximum(high, jnp.max(scores, axis=0, keepdims=True))
                    total = total * jnp.exp(high - new) + jnp.sum(
                        jnp.exp(scores - new), axis=0, keepdims=True
                    )
                    high = new
                col_max[slot] = high
                col_sum[slot] = total

        @pl.loop(0, count)
        def _(slot):
            position = pos_ref[blk * SLOTS + slot]
            old = tab_max[position]
            high = col_max[slot]
            new = jnp.maximum(old, high)
            tab_sum[position] = tab_sum[position] * jnp.exp(old - new) + col_sum[slot] * jnp.exp(
                high - new
            )
            tab_max[position] = new

    sums = tab_sum[...]
    used = sums > 0.0
    part_ref[...] = jnp.where(
        used, tab_max[...] + jnp.log(jnp.where(used, sums, 1.0)), NEG_FILL
    )


def second_kernel(
    pos_ref, cnt_ref, src_ref, logw_ref, fs_ref, dual_ref, loc_ref, dev_ref, grp_ref,
    pot_ref, map_ref, sum_ref,
    held, kept, fs_col, acc, sems,
):
    scale = LOG2E / math.sqrt(EMB)
    rows = src_ref.shape[1]
    fetch_all(pos_ref, cnt_ref, loc_ref, dev_ref, grp_ref, held, sems)
    sum_ref[...] = jnp.zeros_like(sum_ref)

    @pl.loop(0, BLK_DEV)
    def _(blk):
        count = cnt_ref[blk]
        first_source = fs_ref[blk]
        fs_col[...] = as_columns(first_source * LOG2E)
        acc[...] = jnp.zeros_like(acc)

        @pl.loop(0, count)
        def _(slot):
            at = blk * SLOTS + slot
            pltpu.make_async_copy(loc_ref.at[0], held.at[at], sems.at[at]).wait()
            dual = dual_ref[pos_ref[at]] * LOG2E
            points = held[at]
            beside = jnp.concatenate([points, jnp.ones((rows, LANES), jnp.bfloat16)], axis=1)
            for part in range(rows // LANES):
                span = pl.ds(part * LANES, LANES)
                col = fs_col[span, :]
                shift = jnp.concatenate([col] * (rows // LANES), axis=1)
                plan = jnp.exp2(raw_scores(src_ref[blk, span, :], points) * scale + (dual + shift))
                plan = plan.astype(jnp.bfloat16)
                kept[slot, span, :] = plan
                acc[span, :] += jnp.dot(plan, beside, preferred_element_type=jnp.float32)

        row_col = acc[:, LANES:]
        map_ref[blk] = acc[:, :LANES] / row_col
        row_sum = as_row(row_col)
        logw = logw_ref[blk]
        pot_ref[blk] = logw + first_source - jnp.log(row_sum)
        weights = weight_rows(jnp.exp(logw) / row_sum)

        @pl.loop(0, count)
        def _(slot):
            position = pos_ref[blk * SLOTS + slot]
            sum_ref[position] += jnp.sum(
                jnp.dot(weights, kept[slot], preferred_element_type=jnp.float32),
                axis=0,
                keepdims=True,
            )


def greet(dev_count, group_count, me_dev, me_group):
    barrier = pltpu.get_barrier_semaphore()

    def to_dev(step, carry):
        peer = lax.rem(me_dev + step, dev_count)
        pl.semaphore_signal(barrier, inc=1, device_id=(me_group, peer), device_id_type=MESH)
        return carry

    def to_group(step, carry):
        peer = lax.rem(me_group + step, group_count)
        pl.semaphore_signal(barrier, inc=1, device_id=(peer, me_dev), device_id_type=MESH)
        return carry

    lax.fori_loop(1, dev_count, to_dev, 0)
    lax.fori_loop(1, group_count, to_group, 0)
    pl.semaphore_wait(barrier, dev_count + group_count - 2)


def exchange(
    out_ref, out_base, in_ref, in_base, send_sem, recv_sem, dev_count, group_count, me_dev, me_group
):
    def to_dev(step):
        peer = lax.rem(me_dev + step, dev_count)
        return pltpu.make_async_remote_copy(
            src_ref=out_ref.at[out_base + peer],
            dst_ref=in_ref.at[in_base + me_dev],
            send_sem=send_sem.at[step],
            recv_sem=recv_sem.at[step],
            device_id=(me_group, peer),
            device_id_type=MESH,
        )

    def to_group(step):
        peer = lax.rem(me_group + step, group_count)
        return pltpu.make_async_remote_copy(
            src_ref=out_ref.at[out_base + dev_count + peer],
            dst_ref=in_ref.at[in_base + dev_count + me_group],
            send_sem=send_sem.at[dev_count + step],
            recv_sem=recv_sem.at[dev_count + step],
            device_id=(peer, me_dev),
            device_id_type=MESH,
        )

    def start(copy_of):
        def body(step, carry):
            copy_of(step).start()
            return carry

        return body

    def wait(copy_of):
        def body(step, carry):
            copy_of(step).wait()
            return carry

        return body

    lax.fori_loop(1, dev_count, start(to_dev), 0)
    lax.fori_loop(1, group_count, start(to_group), 0)
    lax.fori_loop(1, dev_count, wait(to_dev), 0)
    lax.fori_loop(1, group_count, wait(to_group), 0)


def settle_kernel(
    dev_count, group_count, pick_ref, part_ref, logw_ref, dual_ref,
    inbox, outbox, send_a, recv_a, send_b, recv_b,
):
    me_group, me_dev = lax.axis_index("group"), lax.axis_index("dev")
    blocks = BLK_DEV
    peers = dev_count + group_count
    empty = jnp.full(inbox.shape[1:], NEG_FILL, jnp.float32)
    greet(dev_count, group_count, me_dev, me_group)
    inbox[me_dev] = empty
    inbox[dev_count + me_group] = empty
    exchange(
        part_ref, blocks, inbox, 0, send_a, recv_a, dev_count, group_count, me_dev, me_group
    )
    own = [part_ref[q] for q in range(blocks)]

    def highest(e, carry):
        pick, here = pick_ref[e], inbox[e]
        return tuple(
            jnp.maximum(high, jnp.where(pick == q, here, NEG_FILL)) for q, high in enumerate(carry)
        )

    highs = lax.fori_loop(0, peers, highest, tuple(own))

    def summed(e, carry):
        pick, here = pick_ref[e], inbox[e]
        return tuple(
            total + jnp.exp(jnp.where(pick == q, here, NEG_FILL) - highs[q])
            for q, total in enumerate(carry)
        )

    totals = lax.fori_loop(
        0, peers, summed, tuple(jnp.exp(o - h) for o, h in zip(own, highs))
    )
    duals = [
        logw_ref[q] - (highs[q] + jnp.log(totals[q])) for q in range(blocks)
    ]
    for q in range(blocks):
        dual_ref[q] = duals[q]

    def fill(e, carry):
        pick = pick_ref[e]
        chosen = jnp.zeros_like(duals[0])
        for q in range(blocks):
            chosen = jnp.where(pick == q, duals[q], chosen)
        outbox[e] = chosen
        return carry

    lax.fori_loop(0, peers, fill, 0)
    dual_ref[blocks + me_dev] = jnp.zeros_like(duals[0])
    dual_ref[blocks + dev_count + me_group] = jnp.zeros_like(duals[0])
    exchange(
        outbox, 0, dual_ref, blocks, send_b, recv_b, dev_count, group_count, me_dev, me_group
    )


def close_kernel(
    dev_count, group_count, pick_ref, sum_ref, logw_ref, first_ref, pot_ref, inbox, send_a, recv_a
):
    me_group, me_dev = lax.axis_index("group"), lax.axis_index("dev")
    blocks = BLK_DEV
    peers = dev_count + group_count
    greet(dev_count, group_count, me_dev, me_group)
    inbox[me_dev] = jnp.zeros(inbox.shape[1:], jnp.float32)
    inbox[dev_count + me_group] = jnp.zeros(inbox.shape[1:], jnp.float32)
    exchange(
        sum_ref, blocks, inbox, 0, send_a, recv_a, dev_count, group_count, me_dev, me_group
    )

    def summed(e, carry):
        pick, here = pick_ref[e], inbox[e]
        return tuple(
            total + jnp.where(pick == q, here, 0.0) for q, total in enumerate(carry)
        )

    totals = lax.fori_loop(0, peers, summed, tuple(sum_ref[q] for q in range(blocks)))
    for q in range(blocks):
        pot_ref[q] = logw_ref[q] - jnp.log(totals[q]) + first_ref[q]


def shards(source_points, target_points, source_logw, target_logw, pair_targets, pair_count):
    group_count = lax.axis_size("group")
    dev_count = lax.axis_size("dev")
    group_idx = lax.axis_index("group")
    dev_idx = lax.axis_index("dev")
    myself = group_idx * dev_count + dev_idx
    blocks, rows, slots = BLK_DEV, BLOCK, SLOTS
    table = blocks + dev_count + group_count
    peers = dev_count + group_count
    sources = source_points.reshape(blocks, rows, EMB)
    targets = target_points.reshape(blocks, rows, EMB)
    log_src = source_logw.reshape(blocks, 1, rows)
    log_tgt = target_logw.reshape(blocks, rows // LANES, LANES)

    own_targets = lax.dynamic_slice_in_dim(pair_targets, myself * blocks, blocks, 0)
    own_counts = lax.dynamic_slice_in_dim(pair_count, myself * blocks, blocks, 0)
    owners = own_targets // blocks
    position = jnp.where(
        owners == myself,
        own_targets % blocks,
        jnp.where(
            owners // dev_count == group_idx,
            blocks + owners % dev_count,
            blocks + dev_count + owners // dev_count,
        ),
    ).reshape(blocks * slots)
    everything = pair_targets.reshape(group_count, dev_count, blocks, slots)
    counts_all = pair_count.reshape(group_count, dev_count, blocks)
    pick_dev = requests(
        lax.dynamic_index_in_dim(everything, group_idx, 0, keepdims=False),
        lax.dynamic_index_in_dim(counts_all, group_idx, 0, keepdims=False),
        myself,
        jnp.arange(dev_count, dtype=jnp.int32) == dev_idx,
        blocks,
    )
    pick_grp = requests(
        lax.dynamic_index_in_dim(everything, dev_idx, 1, keepdims=False),
        lax.dynamic_index_in_dim(counts_all, dev_idx, 1, keepdims=False),
        myself,
        jnp.arange(group_count, dtype=jnp.int32) == group_idx,
        blocks,
    )
    pick = jnp.concatenate([pick_dev, pick_grp])
    dev_rows = lax.all_to_all(
        jnp.take(targets, jnp.maximum(pick_dev, 0), axis=0), "dev", 0, 0, tiled=True
    )
    grp_rows = lax.all_to_all(
        jnp.take(targets, jnp.maximum(pick_grp, 0), axis=0), "group", 0, 0, tiled=True
    )

    smem = pl.BlockSpec(memory_space=pltpu.SMEM)
    vmem = pl.BlockSpec(memory_space=pltpu.VMEM)
    anywhere = pl.BlockSpec(memory_space=pl.ANY)
    f32 = jnp.float32
    held = pltpu.VMEM((blocks * slots, rows, EMB), jnp.bfloat16)
    kept = pltpu.VMEM((slots, rows, rows), jnp.bfloat16)
    copy_sems = pltpu.SemaphoreType.DMA((blocks * slots,))
    pairs = blocks * slots

    first_source, part = pl.pallas_call(
        first_kernel,
        out_shape=(
            jax.ShapeDtypeStruct((blocks, 1, rows), f32),
            jax.ShapeDtypeStruct((table, 1, rows), f32),
        ),
        in_specs=[smem, smem, vmem, vmem, anywhere, anywhere, anywhere],
        out_specs=(vmem, vmem),
        scratch_shapes=[
            held,
            kept,
            pltpu.VMEM((rows, LANES), f32),
            pltpu.VMEM((slots, 1, rows), f32),
            pltpu.VMEM((slots, 1, rows), f32),
            pltpu.VMEM((table, 1, rows), f32),
            pltpu.VMEM((table, 1, rows), f32),
            pltpu.VMEM((rows, LANES), f32),
            copy_sems,
        ],
        compiler_params=pltpu.CompilerParams(vmem_limit_bytes=VMEM_LIMIT),
        cost_estimate=pl.CostEstimate(
            flops=4 * pairs * rows * rows * EMB, bytes_accessed=6 * 2**20, transcendentals=pairs * rows * rows
        ),
        name="first_pass",
    )(position, own_counts, sources, log_src, targets, dev_rows, grp_rows)

    small = (rows // LANES, LANES)
    sems = pltpu.SemaphoreType.DMA((peers,))
    dual = pl.pallas_call(
        functools.partial(settle_kernel, dev_count, group_count),
        out_shape=jax.ShapeDtypeStruct((table, *small), f32),
        in_specs=[smem, vmem, vmem],
        out_specs=vmem,
        scratch_shapes=[
            pltpu.VMEM((peers, *small), f32),
            pltpu.VMEM((peers, *small), f32),
            sems,
            sems,
            sems,
            sems,
        ],
        compiler_params=pltpu.CompilerParams(collective_id=0, has_side_effects=True),
        name="settle_first",
    )(pick, part.reshape(table, *small), log_tgt)

    potential, mapped, col_sums = pl.pallas_call(
        second_kernel,
        out_shape=(
            jax.ShapeDtypeStruct((blocks, 1, rows), f32),
            jax.ShapeDtypeStruct((blocks, rows, EMB), f32),
            jax.ShapeDtypeStruct((table, 1, rows), f32),
        ),
        in_specs=[smem, smem, vmem, vmem, vmem, vmem, anywhere, anywhere, anywhere],
        out_specs=(vmem, vmem, vmem),
        scratch_shapes=[
            held,
            kept,
            pltpu.VMEM((rows, LANES), f32),
            pltpu.VMEM((rows, 2 * LANES), f32),
            copy_sems,
        ],
        compiler_params=pltpu.CompilerParams(vmem_limit_bytes=VMEM_LIMIT),
        cost_estimate=pl.CostEstimate(
            flops=8 * pairs * rows * rows * EMB, bytes_accessed=7 * 2**20, transcendentals=pairs * rows * rows
        ),
        name="second_pass",
    )(
        position, own_counts, sources, log_src, first_source,
        dual.reshape(table, 1, rows), targets, dev_rows, grp_rows,
    )

    target_potential = pl.pallas_call(
        functools.partial(close_kernel, dev_count, group_count),
        out_shape=jax.ShapeDtypeStruct((blocks, *small), f32),
        in_specs=[smem, vmem, vmem, vmem],
        out_specs=vmem,
        scratch_shapes=[pltpu.VMEM((peers, *small), f32), sems, sems],
        compiler_params=pltpu.CompilerParams(collective_id=1, has_side_effects=True),
        name="settle_second",
    )(pick, col_sums.reshape(table, *small), log_tgt, dual)
    return (
        potential.reshape(blocks * rows),
        target_potential.reshape(blocks * rows),
        mapped.reshape(blocks * rows, EMB),
    )


def solution(mesh):
    return jax.shard_map(
        shards,
        mesh=mesh,
        in_specs=(
            P(("group", "dev"), None),
            P(("group", "dev"), None),
            P(("group", "dev")),
            P(("group", "dev")),
            P(),
            P(),
        ),
        out_specs=(P(("group", "dev")), P(("group", "dev")), P(("group", "dev"), None)),
        check_vma=False,
    )
```

time: 1980 us -> 163 us (0.08)
  starting transfers between devices: 806 us -> 14.9 us
  loops' own time: 617 us -> 0 us
  local copies, waits for them, and re-layouts: 209 us -> 10.8 us
  other arithmetic: 169 us -> 7.94 us
  Pallas kernels: 0 us -> 79.6 us
  matrix products: 61 us -> 0 us
  waiting for transfers between devices: 99.8 us -> 48 us
    all_to_all x12 -> x2, starting transfers between devices: 806 us -> 14.9 us  [the longest x1 9.9 us: shards(): lax.all_to_all(jnp.take(targets, jnp.maximum(pick_dev, 0), axis=0), 'dev'...]
    another operation x132 -> x0, loops' own time: 617 us -> none  [the longest x2 214 us: row_pass(): (row_high, row_sum), _ = lax.scan(row_advance, start_state, pair_ids)]
    dynamic_slice x341 -> x1, local copies, waits for them, and re-layouts: 187 us -> 0.76 us  [shards(): lax.dynamic_slice_in_dim(pair_count, myself * blocks, blocks, 0)]
    another operation x144 -> x0, other arithmetic: 134 us -> none
    pallas_call x0 -> x4, Pallas kernels: none -> 79.6 us  [the longest x1 31.5 us: shards(): pl.pallas_call(functools.partial(settle_kernel, dev_count, group_count),...]
    dot_general x60 -> x0, matrix products: 61 us -> none  [the longest x48 48.3 us: block_scores(): lax.dot_general(left, right, (((1,), (1,)), ((), ())), preferred_element_...]
    all_to_all x12 -> x2, waiting for transfers between devices: 99.8 us -> 48 us  [the longest x1 48 us: shards(): lax.all_to_all(jnp.take(targets, jnp.maximum(pick_dev, 0), axis=0), 'dev'...]
  transfers between devices with their start and end apart: 12 -> 2, of which waited for: 11 -> 1; matrix products, arithmetic and copies ran while one was open for 1% -> 7% of each run, Pallas kernels for 0% -> 0%
where the time goes in v1:
time: 163 us; the launch traced here: 162 us
  Pallas kernels  79.6 us (49%)
  waiting for transfers between devices  48 us (29%)
  starting transfers between devices  14.9 us (9%)
  local copies, waits for them, and re-layouts  10.8 us (7%)
  other arithmetic  7.94 us (5%)
    all_to_all x1, waiting for transfers between devices, shards(): lax.all_to_all(jnp.take(targets, jnp.maximum(pick_dev, 0), axis=0), 'dev'...  48 us
    pallas_call x1, Pallas kernels, shards(): pl.pallas_call(functools.partial(settle_kernel, dev_count, group_count),...  31.5 us
    pallas_call x1, Pallas kernels, shards(): pl.pallas_call(functools.partial(close_kernel, dev_count, group_count), o...  28.6 us
    pallas_call x1, Pallas kernels, shards(): pl.pallas_call(second_kernel, out_shape=(jax.ShapeDtypeStruct((blocks, 1,...  10.6 us
    all_to_all x1, starting transfers between devices, shards(): lax.all_to_all(jnp.take(targets, jnp.maximum(pick_dev, 0), axis=0), 'dev'...  9.9 us
    pallas_call x1, Pallas kernels, shards(): pl.pallas_call(first_kernel, out_shape=(jax.ShapeDtypeStruct((blocks, 1,...  8.89 us
    all_to_all x1, starting transfers between devices, shards(): lax.all_to_all(jnp.take(targets, jnp.maximum(pick_grp, 0), axis=0), 'grou...  5.01 us
    select_n x1, other arithmetic, shards(): jnp.take(targets, jnp.maximum(pick_dev, 0), axis=0)  4.63 us
  transfers between devices with their start and end apart: 2, of which 1 were waited for; matrix products, arithmetic and copies ran while one was open for 7% of the time, Pallas kernels for 0%

profile of v1, /device:TPU:1, one launch (start us, length us, event | category | flops | bytes accessed | tf_op | source)
XLA Modules:
  0.0 162.0 jit_solution(14406194946541566425)
XLA Ops:
  0.6 0.0 copy-start
  0.6 0.8 reshape.91
  1.5 0.8 copy.16
  2.4 0.2 fusion.9
  2.7 1.7 %gather_fusion.1 = bf16[4,512,128]{2,1,0:T(8,128)(2,1)S(1)} fusion(bf16[4,512,128]{2,1,0:T(8,128)(2,1)} %bitcast.50, s32[1024]{0:T(1024)S(1)} %pad_clamp_fusion), kind=kCustom, calls=%fused_computation.1 | custom fusion | bytes 1048592 | tf_op jit(solution)/shard_map/jit(_take)/gather | solution.py:429
  4.4 0.9 broadcast_select_fusion.1
  5.3 5.0 %all-to-all-start.1 = ((bf16[4,512,128]{2,1,0:T(8,128)(2,1)}), bf16[4,512,128]{2,1,0:T(8,128)(2,1)S(1)}, u32[]{:S(2)}, u32[]{:S(2)}) async-start(bf16[4,512,128]{2,1,0:T(8,128)(2,1)} %broadcast_select_fusion.1), calls=%async_computation.1 | async-start | bytes 1048576 | tf_op jit(solution)/shard_map/all_to_all | solution.py:428
  10.3 0.8 fusion.2
  11.1 0.0 copy-done
  11.1 3.1 %gather_fusion = bf16[32,512,128]{2,1,0:T(8,128)(2,1)} fusion(bf16[4,512,128]{2,1,0:T(8,128)(2,1)S(1)} %bitcast.51, s32[1024]{0:T(1024)S(1)} %pad_clamp_fusion.1), kind=kCustom, calls=%fused_computation | custom fusion | bytes 8388736 | tf_op jit(solution)/shard_map/jit(_take)/gather | solution.py:426
  14.2 4.6 %broadcast_select_fusion = bf16[32,512,128]{2,1,0:T(8,128)(2,1)} fusion(bf16[32,512,128]{2,1,0:T(8,128)(2,1)} %gather_fusion, pred[32]{0:T(512)(128)(4,1)S(1)} %broadcast_compare_fusion.1), kind=kLoop, calls=%fused_computation.2 | loop fusion | flops 2097152 | bytes 8388640 | tf_op jit(solution)/shard_map/jit(_take)/select_n | solution.py:426
  18.8 0.0 copy-start.4
  18.8 0.0 copy-start.5
  18.8 0.0 all-to-all-done.1.grp_ref
  18.8 9.9 %all-to-all-start = ((bf16[32,512,128]{2,1,0:T(8,128)(2,1)}), bf16[32,512,128]{2,1,0:T(8,128)(2,1)}, u32[]{:S(2)}, u32[]{:S(2)}) async-start(bf16[32,512,128]{2,1,0:T(8,128)(2,1)} %broadcast_select_fusion), calls=%async_computation | async-start | bytes 8388608 | tf_op jit(solution)/shard_map/all_to_all | solution.py:425
  28.7 0.8 dynamic_slice.23.cnt_ref
  29.5 0.8 fusion.14
  30.2 0.1 copy.13
  30.3 0.1 reshape.87.pos_ref
  30.4 0.6 pad_add_fusion.pick_ref
  31.0 48.0 %all-to-all-done.dev_ref = bf16[32,512,128]{2,1,0:T(8,128)(2,1)} async-done(((bf16[32,512,128]{2,1,0:T(8,128)(2,1)}), bf16[32,512,128]{2,1,0:T(8,128)(2,1)}, u32[]{:S(2)}, u32[]{:S(2)}) %all-to-all-start) | async-done | bytes 4194336 | tf_op jit(solution)/shard_map/all_to_all | solution.py:425
  79.0 0.0 copy-done.4
  79.0 0.0 copy-done.5
  79.0 8.9 %first_pass.1 = (f32[4,1,512]{2,1,0:T(1,128)S(1)}, f32[40,1,512]{2,1,0:T(1,128)S(1)}) custom-call(s32[32]{0:T(128)S(1)} %reshape.87.pos_ref, s32[4]{0:T(128)S(1)} %dynamic_slice.23.cnt_ref, bf16[4,512,128]{2,1,0:T(8,128)(2,1)S(1)} %bitcast.57, f32[4,1,512]{2,1,0:T(1,128)S(1)} %bitcast.59, bf16[4,512,128]{2,1,0:T(8,128)(2,1)S(1)} %bitcast.52, ...), custom_call_target="tpu_custom_call" | custom-call | flops 4294967296 | bytes 6291456 | tf_op jit(solution)/shard_map/first_pass/pallas_call | solution.py:441
  87.9 0.0 copy-start.3
  87.9 0.6 copy-done.3
  88.5 31.5 %settle_first.1.first_ref = f32[40,4,128]{2,1,0:T(4,128)} custom-call(s32[36]{0:T(128)} %pad_add_fusion.pick_ref, f32[40,4,128]{2,1,0:T(4,128)} %bitcast.56, f32[4,4,128]{2,1,0:T(4,128)} %bitcast.64), custom_call_target="tpu_custom_call" | custom-call | tf_op jit(solution)/shard_map/settle_first/pallas_call | solution.py:469
  120.0 0.0 copy-start.1
  120.0 0.9 copy-done.1
  120.9 10.6 %second_pass.1 = (f32[4,1,512]{2,1,0:T(1,128)}, f32[4,512,128]{2,1,0:T(8,128)}, f32[40,1,512]{2,1,0:T(1,128)S(1)}) custom-call(s32[32]{0:T(128)S(1)} %reshape.87.pos_ref, s32[4]{0:T(128)S(1)} %dynamic_slice.23.cnt_ref, bf16[4,512,128]{2,1,0:T(8,128)(2,1)S(1)} %bitcast.58, f32[4,1,512]{2,1,0:T(1,128)S(1)} %bitcast.60, ...), custom_call_target="tpu_custom_call" | custom-call | flops 8589934592 | bytes 7340032 | tf_op jit(solution)/shard_map/second_pass/pallas_call | solution.py:486
  131.5 0.0 copy-start.2
  131.5 0.6 copy-done.2
  132.2 28.6 %settle_second.1 = f32[4,4,128]{2,1,0:T(4,128)} custom-call(s32[36]{0:T(128)} %pad_add_fusion.pick_ref, f32[40,4,128]{2,1,0:T(4,128)} %bitcast.55, f32[4,4,128]{2,1,0:T(4,128)} %bitcast.65, f32[40,4,128]{2,1,0:T(4,128)} %settle_first.1.first_ref), custom_call_target="tpu_custom_call" | custom-call | tf_op jit(solution)/shard_map/settle_second/pallas_call | solution.py:512
  160.7 1.3 copy.19
  (10 shorter events, 0.1 us)
Async XLA Ops:
  0.6 10.5 %copy-start = (bf16[2048,128]{1,0:T(8,128)(2,1)S(1)}, bf16[2048,128]{1,0:T(8,128)(2,1)}, u32[]{:S(2)}) copy-start(bf16[2048,128]{1,0:T(8,128)(2,1)} %param.7) | copy-start | bytes 1572868
  5.3 13.5 %all-to-all-start.1 = ((bf16[4,512,128]{2,1,0:T(8,128)(2,1)}), bf16[4,512,128]{2,1,0:T(8,128)(2,1)S(1)}, u32[]{:S(2)}, u32[]{:S(2)}) async-start(bf16[4,512,128]{2,1,0:T(8,128)(2,1)} %broadcast_select_fusion.1), calls=%async_computation.1 | async-start | bytes 1048576 | tf_op jit(solution)/shard_map/all_to_all | solution.py:428
  18.8 60.2 %copy-start.4 = (bf16[2048,128]{1,0:T(8,128)(2,1)S(1)}, bf16[2048,128]{1,0:T(8,128)(2,1)}, u32[]{:S(2)}) copy-start(bf16[2048,128]{1,0:T(8,128)(2,1)} %param.6) | copy-start | bytes 1572868
  18.8 60.2 %copy-start.5 = (f32[2048]{0:T(1024)S(1)}, f32[2048]{0:T(1024)}, u32[]{:S(2)}) copy-start(f32[2048]{0:T(1024)} %param.8) | copy-start | bytes 24580
  18.8 60.2 %all-to-all-start = ((bf16[32,512,128]{2,1,0:T(8,128)(2,1)}), bf16[32,512,128]{2,1,0:T(8,128)(2,1)}, u32[]{:S(2)}, u32[]{:S(2)}) async-start(bf16[32,512,128]{2,1,0:T(8,128)(2,1)} %broadcast_select_fusion), calls=%async_computation | async-start | bytes 8388608 | tf_op jit(solution)/shard_map/all_to_all | solution.py:425
  87.9 0.6 copy-start.3
  120.0 0.9 copy-start.1
  131.5 0.6 copy-start.2

commit v2 on v1

--- a/solution.py
+++ b/solution.py
@@ -20,11 +20,17 @@
 VMEM_LIMIT = 48 * 2**20
 
 
-def requests(targets, counts, owner_self, skipped, blk_count):
-    slot_count = targets.shape[2]
-    active = jnp.arange(slot_count, dtype=jnp.int32)[None, None, :] < counts[:, :, None]
-    match = active & (targets // blk_count == owner_self) & jnp.logical_not(skipped)[:, None, None]
-    return jnp.max(jnp.where(match, targets % blk_count, -1), axis=(1, 2))
+RING = 4
+TRUNK = (0, 3, 1, 2)
+BRANCH = ((2, 0), (2, 1), (1, 0), (1, 1), (3, 0), (3, 1))
+
+
+def chosen_blocks(targets, counts, first, sources):
+    takers, blocks, slots = targets.shape
+    active = jnp.arange(slots, dtype=jnp.int32) < counts[:, :, None]
+    named = jnp.where(active, targets - first, -1).reshape(takers, blocks * slots, 1)
+    match = (named >= 0) & (named // blocks == sources)
+    return jnp.max(jnp.where(match, named % blocks, -1), axis=1)
 
 
 def raw_scores(left, right):
@@ -50,62 +56,80 @@
     return rows.astype(jnp.bfloat16)
 
 
-def fetch_all(pos_ref, cnt_ref, loc_ref, dev_ref, grp_ref, held, sems):
-    blocks, slots = BLK_DEV, SLOTS
-    dev_count = dev_ref.shape[0]
-
-    @pl.loop(0, blocks * slots)
+def fetch_all(pos_ref, cnt_ref, loc_ref, tab_ref, held, sems, clear):
+    @pl.loop(0, BLK_DEV * SLOTS)
     def _(at):
         position = pos_ref[at]
-        active = lax.rem(at, slots) < cnt_ref[at // slots]
-
-        @pl.when(active & (position < blocks))
+        active = lax.rem(at, SLOTS) < cnt_ref[at // SLOTS]
+
+        @pl.when(active & (position < BLK_DEV))
         def _():
             pltpu.make_async_copy(loc_ref.at[position], held.at[at], sems.at[at]).start()
 
-        @pl.when(active & (position >= blocks) & (position < blocks + dev_count))
+        @pl.when(active & (position >= BLK_DEV))
         def _():
-            pltpu.make_async_copy(dev_ref.at[position - blocks], held.at[at], sems.at[at]).start()
-
-        @pl.when(active & (position >= blocks + dev_count))
-        def _():
-            pltpu.make_async_copy(
-                grp_ref.at[position - blocks - dev_count], held.at[at], sems.at[at]
-            ).start()
+            pltpu.make_async_copy(tab_ref.at[position], held.at[at], sems.at[at]).start()
+
+        if clear:
+
+            @pl.when(jnp.logical_not(active))
+            def _():
+                held[at] = jnp.zeros(held.shape[1:], held.dtype)
+
+
+def await_blocks(blk, count, loc_ref, held, sems):
+    @pl.loop(0, count)
+    def _(slot):
+        at = blk * SLOTS + slot
+        pltpu.make_async_copy(loc_ref.at[0], held.at[at], sems.at[at]).wait()
+
+
+def by_width(count, work):
+    @pl.when(count <= SLOTS // 2)
+    def _():
+        work(SLOTS // 2)
+
+    @pl.when(count > SLOTS // 2)
+    def _():
+        work(SLOTS)
+
+
+def column_sums(weights, kept, slot):
+    return jnp.sum(
+        jnp.dot(weights, kept[slot], preferred_element_type=jnp.float32), axis=0, keepdims=True
+    )
 
 
 def first_kernel(
-    pos_ref, cnt_ref, src_ref, logw_ref, loc_ref, dev_ref, grp_ref,
+    pos_ref, cnt_ref, src_ref, logw_ref, loc_ref, tab_ref,
     fs_ref, part_ref,
     held, kept, row_acc, col_max, col_sum, tab_max, tab_sum, col_tmp, sems,
 ):
     factor = 1.0 / math.sqrt(EMB)
     scale = factor * LOG2E
     rows = src_ref.shape[1]
-    fetch_all(pos_ref, cnt_ref, loc_ref, dev_ref, grp_ref, held, sems)
+    fetch_all(pos_ref, cnt_ref, loc_ref, tab_ref, held, sems, False)
     tab_max[...] = jnp.full_like(tab_max, NEG_FILL)
     tab_sum[...] = jnp.zeros_like(tab_sum)
 
     @pl.loop(0, BLK_DEV)
     def _(blk):
         count = cnt_ref[blk]
-        row_acc[...] = jnp.zeros_like(row_acc)
+        await_blocks(blk, count, loc_ref, held, sems)
         col_max[...] = jnp.zeros_like(col_max)
-        col_sum[...] = jnp.ones_like(col_sum)
-
-        @pl.loop(0, count)
-        def _(slot):
-            at = blk * SLOTS + slot
-            pltpu.make_async_copy(loc_ref.at[0], held.at[at], sems.at[at]).wait()
-            for part in range(rows // LANES):
-                span = pl.ds(part * LANES, LANES)
-                kern = jnp.exp2(raw_scores(src_ref[blk, span, :], held[at]) * scale)
+
+        def row_work(width):
+            totals = jnp.zeros_like(row_acc)
+            for slot in range(width):
+                kern = jnp.exp2(raw_scores(src_ref[blk], held[blk * SLOTS + slot]) * scale)
+                kept[slot] = kern.astype(jnp.bfloat16)
                 total = kern[:, :LANES]
                 for lane in range(1, rows // LANES):
                     total = total + kern[:, lane * LANES : (lane + 1) * LANES]
-                row_acc[span, :] += total
-                kept[slot, span, :] = kern.astype(jnp.bfloat16)
-
+                totals = totals + jnp.where(slot < count, total, 0.0)
+            row_acc[...] = totals
+
+        by_width(count, row_work)
         row_sum = lax.dot_general(
             jnp.ones((8, LANES), jnp.float32),
             row_acc[...],
@@ -117,18 +141,16 @@
         fs_ref[blk] = logw - jnp.log(row_sum)
         weights = weight_rows(jnp.exp(logw) / row_sum)
 
-        @pl.loop(0, count)
-        def _(slot):
-            col_sum[slot] = jnp.sum(
-                jnp.dot(weights, kept[slot], preferred_element_type=jnp.float32),
-                axis=0,
-                keepdims=True,
-            )
-
+        def column_work(width):
+            for slot in range(width):
+                col_sum[slot] = column_sums(weights, kept, slot)
+
+        by_width(count, column_work)
         row_fine = (row_sum >= ROW_LOW) & (row_sum <= ROW_HIGH)
-        fine = jnp.min(jnp.where(row_fine, 1.0, 0.0))
-        col_fine = jnp.where(col_sum[...] >= COL_LOW, 1.0, 0.0)
-        fine = jnp.minimum(fine, jnp.min(jnp.min(col_fine, axis=0)))
+        slot_at = lax.broadcasted_iota(jnp.int32, col_sum.shape, 0)
+        col_fine = (slot_at >= count) | (col_sum[...] >= COL_LOW)
+        fine = jnp.min(jnp.where(col_fine, 1.0, 0.0), axis=0)
+        fine = jnp.min(jnp.where(row_fine, fine, 0.0))
 
         @pl.when(fine < 0.5)
         def _():
@@ -187,38 +209,40 @@
 
 
 def second_kernel(
-    pos_ref, cnt_ref, src_ref, logw_ref, fs_ref, dual_ref, loc_ref, dev_ref, grp_ref,
+    pos_ref, cnt_ref, src_ref, logw_ref, fs_ref, dual_ref, loc_ref, tab_ref,
     pot_ref, map_ref, sum_ref,
     held, kept, fs_col, acc, sems,
 ):
     scale = LOG2E / math.sqrt(EMB)
     rows = src_ref.shape[1]
-    fetch_all(pos_ref, cnt_ref, loc_ref, dev_ref, grp_ref, held, sems)
+    fetch_all(pos_ref, cnt_ref, loc_ref, tab_ref, held, sems, True)
     sum_ref[...] = jnp.zeros_like(sum_ref)
+    ones = jnp.ones((rows, LANES), jnp.bfloat16)
 
     @pl.loop(0, BLK_DEV)
     def _(blk):
         count = cnt_ref[blk]
+        await_blocks(blk, count, loc_ref, held, sems)
         first_source = fs_ref[blk]
         fs_col[...] = as_columns(first_source * LOG2E)
         acc[...] = jnp.zeros_like(acc)
 
-        @pl.loop(0, count)
-        def _(slot):
-            at = blk * SLOTS + slot
-            pltpu.make_async_copy(loc_ref.at[0], held.at[at], sems.at[at]).wait()
-            dual = dual_ref[pos_ref[at]] * LOG2E
-            points = held[at]
-            beside = jnp.concatenate([points, jnp.ones((rows, LANES), jnp.bfloat16)], axis=1)
-            for part in range(rows // LANES):
-                span = pl.ds(part * LANES, LANES)
-                col = fs_col[span, :]
-                shift = jnp.concatenate([col] * (rows // LANES), axis=1)
-                plan = jnp.exp2(raw_scores(src_ref[blk, span, :], points) * scale + (dual + shift))
-                plan = plan.astype(jnp.bfloat16)
-                kept[slot, span, :] = plan
-                acc[span, :] += jnp.dot(plan, beside, preferred_element_type=jnp.float32)
-
+        def row_work(width):
+            for slot in range(width):
+                at = blk * SLOTS + slot
+                dual = jnp.where(slot < count, dual_ref[pos_ref[at]] * LOG2E, NEG_FILL)
+                points = held[at]
+                beside = jnp.concatenate([points, ones], axis=1)
+                for part in range(rows // LANES):
+                    span = pl.ds(part * LANES, LANES)
+                    shift = jnp.concatenate([fs_col[span, :]] * (rows // LANES), axis=1)
+                    plan = jnp.exp2(
+                        raw_scores(src_ref[blk, span, :], points) * scale + (dual + shift)
+                    ).astype(jnp.bfloat16)
+                    kept[slot, span, :] = plan
+                    acc[span, :] += jnp.dot(plan, beside, preferred_element_type=jnp.float32)
+
+        by_width(count, row_work)
         row_col = acc[:, LANES:]
         map_ref[blk] = acc[:, :LANES] / row_col
         row_sum = as_row(row_col)
@@ -226,14 +250,160 @@
         pot_ref[blk] = logw + first_source - jnp.log(row_sum)
         weights = weight_rows(jnp.exp(logw) / row_sum)
 
-        @pl.loop(0, count)
-        def _(slot):
-            position = pos_ref[blk * SLOTS + slot]
-            sum_ref[position] += jnp.sum(
-                jnp.dot(weights, kept[slot], preferred_element_type=jnp.float32),
-                axis=0,
-                keepdims=True,
+        def column_work(width):
+            for slot in range(width):
+                position = pos_ref[blk * SLOTS + slot]
+                here = column_sums(weights, kept, slot)
+                sum_ref[position] += jnp.where(slot < count, here, 0.0)
+
+        by_width(count, column_work)
+
+
+def deliver_kernel(
+    dev_count, group_count, pick_ref, grp_ref, tgt_ref, tab_ref,
+    prev_buf, next_buf, far_buf, relay_up, relay_down, stage,
+    trunk_send, trunk_recv, stage_send, tab_recv, relay_recv, fwd_send, grp_recv,
+):
+    me_group, me_dev = lax.axis_index("group"), lax.axis_index("dev")
+    core = lax.rem(me_dev, 2)
+    at_x, at_z = lax.rem(me_dev // 2, RING), me_dev // (2 * RING)
+    half = BLK_DEV // 2
+
+    def device(along, across, to_core):
+        dz = along + core * (across - along)
+        dx = across + core * (along - across)
+        return (lax.rem(at_z + dz, RING) * RING + lax.rem(at_x + dx, RING)) * 2 + to_core
+
+    def send(src, dst, send_sem, recv_sem, dev, group=None):
+        return pltpu.make_async_remote_copy(
+            src_ref=src,
+            dst_ref=dst,
+            send_sem=send_sem,
+            recv_sem=recv_sem,
+            device_id=(me_group if group is None else group, dev),
+            device_id_type=MESH,
+        )
+
+    barrier = pltpu.get_barrier_semaphore()
+    near = [
+        device(i, j, cc) for i, j in ((1, 0), (3, 0), (0, 1), (0, 3)) for cc in (0, 1)
+    ] + [device(0, 0, 1 - core)]
+    for dev in near:
+        pl.semaphore_signal(barrier, inc=1, device_id=(me_group, dev), device_id_type=MESH)
+    for step in range(1, group_count):
+        pl.semaphore_signal(
+            barrier,
+            inc=1,
+            device_id=(lax.rem(me_group + step, group_count), me_dev),
+            device_id_type=MESH,
+        )
+    pl.semaphore_wait(barrier, len(near) + group_count - 1)
+
+    low, top = pl.ds(0, half), pl.ds(half, half)
+    ahead, behind = device(1, 0, core), device(3, 0, core)
+
+    def trunk(n, src, dst, span, dev):
+        return send(src.at[span], dst.at[span], trunk_send.at[n], trunk_recv.at[n], dev)
+
+    trunks = [
+        trunk(0, tgt_ref, prev_buf, low, ahead),
+        trunk(1, tgt_ref, next_buf, top, behind),
+        trunk(2, tgt_ref, prev_buf, top, ahead),
+        trunk(3, tgt_ref, next_buf, low, behind),
+        trunk(4, prev_buf, far_buf, low, ahead),
+        trunk(5, next_buf, far_buf, top, behind),
+    ]
+    for n in range(4):
+        trunks[n].start()
+    sent = []
+
+    def branch(k, buf):
+        source = device(TRUNK[k], 0, core)
+        for n, (across, to_core) in enumerate(BRANCH + ((0, 1 - core),)):
+            taker = device(0, across, to_core)
+            at = k * (len(BRANCH) + 1) + n
+            stage[at] = buf[jnp.maximum(pick_ref[taker, source], 0)]
+            if across == 2:
+                relay, over = ((relay_up, 1), (relay_down, 3))[to_core]
+                which = relay_recv.at[to_core * RING + k]
+                copy = send(
+                    stage.at[at], relay.at[k], stage_send.at[at], which, device(0, over, core)
+                )
+            else:
+                copy = send(
+                    stage.at[at],
+                    tab_ref.at[BLK_DEV + source],
+                    stage_send.at[at],
+                    tab_recv.at[source],
+                    taker,
+                )
+            copy.start()
+            sent.append(copy)
+        if k > 0:
+            at = RING * (len(BRANCH) + 1) + group_count - 1 + k - 1
+            stage[at] = buf[jnp.maximum(pick_ref[me_dev, source], 0)]
+            pltpu.make_async_copy(
+                stage.at[at], tab_ref.at[BLK_DEV + source], tab_recv.at[source]
+            ).start()
+
+    def pass_on(k):
+        for way, (relay, back, over) in enumerate(((relay_up, 3, 1), (relay_down, 1, 3))):
+            source = device(TRUNK[k], back, core)
+            at = way * RING + k
+            copy = send(
+                relay.at[k],
+                tab_ref.at[BLK_DEV + source],
+                fwd_send.at[at],
+                tab_recv.at[source],
+                device(0, over, way),
             )
+            send(
+                relay.at[k], relay.at[k], fwd_send.at[at], relay_recv.at[at], ahead
+            ).wait_recv()
+            copy.start()
+            sent.append(copy)
+
+    branch(0, tgt_ref)
+    from_groups = []
+    for step in range(1, group_count):
+        peer = lax.rem(me_group + step, group_count)
+        at = RING * (len(BRANCH) + 1) + step - 1
+        stage[at] = tgt_ref[jnp.maximum(grp_ref[peer], 0)]
+        copy = send(
+            stage.at[at],
+            tab_ref.at[BLK_DEV + dev_count + me_group],
+            stage_send.at[at],
+            grp_recv.at[step],
+            me_dev,
+            peer,
+        )
+        copy.start()
+        sent.append(copy)
+        from_groups.append(copy)
+    trunks[0].wait_recv()
+    trunks[4].start()
+    trunks[1].wait_recv()
+    trunks[5].start()
+    trunks[2].wait_recv()
+    branch(1, prev_buf)
+    trunks[3].wait_recv()
+    branch(2, next_buf)
+    pass_on(0)
+    trunks[4].wait_recv()
+    trunks[5].wait_recv()
+    branch(3, far_buf)
+    pass_on(1)
+    pass_on(2)
+    pass_on(3)
+    for copy in sent + trunks:
+        copy.wait_send()
+    for step in range(1, dev_count):
+        source = lax.rem(me_dev + step, dev_count)
+        send(
+            stage.at[0], tab_ref.at[BLK_DEV + source], stage_send.at[0], tab_recv.at[source], ahead
+        ).wait_recv()
+    for copy in from_groups:
+        copy.wait_recv()
 
 
 def greet(dev_count, group_count, me_dev, me_group):
@@ -299,8 +469,16 @@
     lax.fori_loop(1, group_count, wait(to_group), 0)
 
 
+def picker(pick_ref, grp_ref, dev_count, me_dev):
+    def pick_of(e):
+        of_dev = pick_ref[jnp.minimum(e, dev_count - 1), me_dev]
+        return jnp.where(e < dev_count, of_dev, grp_ref[jnp.maximum(e - dev_count, 0)])
+
+    return pick_of
+
+
 def settle_kernel(
-    dev_count, group_count, pick_ref, part_ref, logw_ref, dual_ref,
+    dev_count, group_count, pick_ref, grp_ref, part_ref, logw_ref, dual_ref,
     inbox, outbox, send_a, recv_a, send_b, recv_b,
 ):
     me_group, me_dev = lax.axis_index("group"), lax.axis_index("dev")
@@ -315,8 +493,10 @@
     )
     own = [part_ref[q] for q in range(blocks)]
 
+    pick_of = picker(pick_ref, grp_ref, dev_count, me_dev)
+
     def highest(e, carry):
-        pick, here = pick_ref[e], inbox[e]
+        pick, here = pick_of(e), inbox[e]
         return tuple(
             jnp.maximum(high, jnp.where(pick == q, here, NEG_FILL)) for q, high in enumerate(carry)
         )
@@ -324,7 +504,7 @@
     highs = lax.fori_loop(0, peers, highest, tuple(own))
 
     def summed(e, carry):
-        pick, here = pick_ref[e], inbox[e]
+        pick, here = pick_of(e), inbox[e]
         return tuple(
             total + jnp.exp(jnp.where(pick == q, here, NEG_FILL) - highs[q])
             for q, total in enumerate(carry)
@@ -340,7 +520,7 @@
         dual_ref[q] = duals[q]
 
     def fill(e, carry):
-        pick = pick_ref[e]
+        pick = pick_of(e)
         chosen = jnp.zeros_like(duals[0])
         for q in range(blocks):
             chosen = jnp.where(pick == q, duals[q], chosen)
@@ -356,7 +536,8 @@
 
 
 def close_kernel(
-    dev_count, group_count, pick_ref, sum_ref, logw_ref, first_ref, pot_ref, inbox, send_a, recv_a
+    dev_count, group_count, pick_ref, grp_ref, sum_ref, logw_ref, first_ref, pot_ref,
+    inbox, send_a, recv_a,
 ):
     me_group, me_dev = lax.axis_index("group"), lax.axis_index("dev")
     blocks = BLK_DEV
@@ -368,8 +549,10 @@
         sum_ref, blocks, inbox, 0, send_a, recv_a, dev_count, group_count, me_dev, me_group
     )
 
+    pick_of = picker(pick_ref, grp_ref, dev_count, me_dev)
+
     def summed(e, carry):
-        pick, here = pick_ref[e], inbox[e]
+        pick, here = pick_of(e), inbox[e]
         return tuple(
             total + jnp.where(pick == q, here, 0.0) for q, total in enumerate(carry)
         )
@@ -407,27 +590,22 @@
     ).reshape(blocks * slots)
     everything = pair_targets.reshape(group_count, dev_count, blocks, slots)
     counts_all = pair_count.reshape(group_count, dev_count, blocks)
-    pick_dev = requests(
+    pick = chosen_blocks(
         lax.dynamic_index_in_dim(everything, group_idx, 0, keepdims=False),
         lax.dynamic_index_in_dim(counts_all, group_idx, 0, keepdims=False),
-        myself,
-        jnp.arange(dev_count, dtype=jnp.int32) == dev_idx,
-        blocks,
-    )
-    pick_grp = requests(
+        group_idx * dev_count * blocks,
+        jnp.arange(dev_count, dtype=jnp.int32),
+    )
+    pick_grp = chosen_blocks(
         lax.dynamic_index_in_dim(everything, dev_idx, 1, keepdims=False),
         lax.dynamic_index_in_dim(counts_all, dev_idx, 1, keepdims=False),
-        myself,
-        jnp.arange(group_count, dtype=jnp.int32) == group_idx,
-        blocks,
-    )
-    pick = jnp.concatenate([pick_dev, pick_grp])
-    dev_rows = lax.all_to_all(
-        jnp.take(targets, jnp.maximum(pick_dev, 0), axis=0), "dev", 0, 0, tiled=True
-    )
-    grp_rows = lax.all_to_all(
-        jnp.take(targets, jnp.maximum(pick_grp, 0), axis=0), "group", 0, 0, tiled=True
-    )
+        myself * blocks,
+        jnp.zeros((1,), jnp.int32),
+    )[:, 0]
+    pick = jnp.where(
+        jnp.arange(dev_count)[:, None] == jnp.arange(dev_count)[None, :], -1, pick
+    )
+    pick_grp = jnp.where(jnp.arange(group_count) == group_idx, -1, pick_grp)
 
     smem = pl.BlockSpec(memory_space=pltpu.SMEM)
     vmem = pl.BlockSpec(memory_space=pltpu.VMEM)
@@ -437,6 +615,31 @@
     kept = pltpu.VMEM((slots, rows, rows), jnp.bfloat16)
     copy_sems = pltpu.SemaphoreType.DMA((blocks * slots,))
     pairs = blocks * slots
+    dma = pltpu.SemaphoreType.DMA
+    block = (rows, EMB)
+    lots = RING * (len(BRANCH) + 1) + group_count - 1 + RING - 1
+    delivered = pl.pallas_call(
+        functools.partial(deliver_kernel, dev_count, group_count),
+        out_shape=jax.ShapeDtypeStruct((table, *block), jnp.bfloat16),
+        in_specs=[smem, smem, vmem],
+        out_specs=anywhere,
+        scratch_shapes=[pltpu.VMEM((blocks, *block), jnp.bfloat16)] * 3
+        + [pltpu.VMEM((RING, *block), jnp.bfloat16)] * 2
+        + [
+            pltpu.VMEM((lots, *block), jnp.bfloat16),
+            dma((6,)),
+            dma((6,)),
+            dma((lots,)),
+            dma((dev_count,)),
+            dma((2 * RING,)),
+            dma((2 * RING,)),
+            dma((group_count,)),
+        ],
+        compiler_params=pltpu.CompilerParams(
+            collective_id=2, has_side_effects=True, vmem_limit_bytes=VMEM_LIMIT
+        ),
+        name="deliver_blocks",
+    )(pick, pick_grp, targets)
 
     first_source, part = pl.pallas_call(
         first_kernel,
@@ -444,7 +647,7 @@
             jax.ShapeDtypeStruct((blocks, 1, rows), f32),
             jax.ShapeDtypeStruct((table, 1, rows), f32),
         ),
-        in_specs=[smem, smem, vmem, vmem, anywhere, anywhere, anywhere],
+        in_specs=[smem, smem, vmem, vmem, anywhere, anywhere],
         out_specs=(vmem, vmem),
         scratch_shapes=[
             held,
@@ -462,14 +665,14 @@
             flops=4 * pairs * rows * rows * EMB, bytes_accessed=6 * 2**20, transcendentals=pairs * rows * rows
         ),
         name="first_pass",
-    )(position, own_counts, sources, log_src, targets, dev_rows, grp_rows)
+    )(position, own_counts, sources, log_src, targets, delivered)
 
     small = (rows // LANES, LANES)
     sems = pltpu.SemaphoreType.DMA((peers,))
     dual = pl.pallas_call(
         functools.partial(settle_kernel, dev_count, group_count),
         out_shape=jax.ShapeDtypeStruct((table, *small), f32),
-        in_specs=[smem, vmem, vmem],
+        in_specs=[smem, smem, vmem, vmem],
         out_specs=vmem,
         scratch_shapes=[
             pltpu.VMEM((peers, *small), f32),
@@ -481,7 +684,7 @@
         ],
         compiler_params=pltpu.CompilerParams(collective_id=0, has_side_effects=True),
         name="settle_first",
-    )(pick, part.reshape(table, *small), log_tgt)
+    )(pick, pick_grp, part.reshape(table, *small), log_tgt)
 
     potential, mapped, col_sums = pl.pallas_call(
         second_kernel,
@@ -490,7 +693,7 @@
             jax.ShapeDtypeStruct((blocks, rows, EMB), f32),
             jax.ShapeDtypeStruct((table, 1, rows), f32),
         ),
-        in_specs=[smem, smem, vmem, vmem, vmem, vmem, anywhere, anywhere, anywhere],
+        in_specs=[smem, smem, vmem, vmem, vmem, vmem, anywhere, anywhere],
         out_specs=(vmem, vmem, vmem),
         scratch_shapes=[
             held,
@@ -506,18 +709,18 @@
         name="second_pass",
     )(
         position, own_counts, sources, log_src, first_source,
-        dual.reshape(table, 1, rows), targets, dev_rows, grp_rows,
+        dual.reshape(table, 1, rows), targets, delivered,
     )
 
     target_potential = pl.pallas_call(
         functools.partial(close_kernel, dev_count, group_count),
         out_shape=jax.ShapeDtypeStruct((blocks, *small), f32),
-        in_specs=[smem, vmem, vmem, vmem],
+        in_specs=[smem, smem, vmem, vmem, vmem],
         out_specs=vmem,
         scratch_shapes=[pltpu.VMEM((peers, *small), f32), sems, sems],
         compiler_params=pltpu.CompilerParams(collective_id=1, has_side_effects=True),
         name="settle_second",
-    )(pick, col_sums.reshape(table, *small), log_tgt, dual)
+    )(pick, pick_grp, col_sums.reshape(table, *small), log_tgt, dual)
     return (
         potential.reshape(blocks * rows),
         target_potential.reshape(blocks * rows),

time: 163 us -> 126 us (0.77)
  waiting for transfers between devices: 48 us -> 0 us
  Pallas kernels: 79.6 us -> 113 us
  starting transfers between devices: 14.9 us -> 0 us
  other arithmetic: 7.94 us -> 1.55 us
    all_to_all x2 -> x0, waiting for transfers between devices: 48 us -> none  [the longest x1 48 us: shards(): lax.all_to_all(jnp.take(targets, jnp.maximum(pick_dev, 0), axis=0), 'dev'...]
    pallas_call x0 -> x1, Pallas kernels: none -> 41.8 us  [shards(): pl.pallas_call(functools.partial(deliver_kernel, dev_count, group_count),...]
    pallas_call x1, Pallas kernels: 28.6 us -> 11 us  [shards(): pl.pallas_call(functools.partial(close_kernel, dev_count, group_count), o...]
    all_to_all x2 -> x0, starting transfers between devices: 14.9 us -> none  [the longest x1 9.9 us: shards(): lax.all_to_all(jnp.take(targets, jnp.maximum(pick_dev, 0), axis=0), 'dev'...]
    pallas_call x1, Pallas kernels: 10.6 us -> 17.2 us  [shards(): pl.pallas_call(second_kernel, out_shape=(jax.ShapeDtypeStruct((blocks, 1,...]
    select_n x2 -> x3, other arithmetic: 5.53 us -> 0.03 us  [the longest x1 0.02 us: chosen_blocks(): match = (named >= 0) & (named // blocks == sources)]
    gather x2 -> x0, local copies, waits for them, and re-layouts: 4.75 us -> none  [the longest x1 3.06 us: shards(): jnp.take(targets, jnp.maximum(pick_dev, 0), axis=0)]
    pallas_call x1, Pallas kernels: 8.89 us -> 12.8 us  [shards(): pl.pallas_call(first_kernel, out_shape=(jax.ShapeDtypeStruct((blocks, 1,...]
  transfers between devices with their start and end apart: 2 -> 0, of which waited for: 1 -> 0; matrix products, arithmetic and copies ran while one was open for 7% -> 0% of each run, Pallas kernels for 0% -> 0%
where the time goes in v2:
time: 126 us; the launch traced here: 125 us
  Pallas kernels  113 us (90%)
  local copies, waits for them, and re-layouts  10.1 us (8%)
  other arithmetic  1.55 us (1%)
    pallas_call x1, Pallas kernels, shards(): pl.pallas_call(functools.partial(deliver_kernel, dev_count, group_count),...  41.8 us
    pallas_call x1, Pallas kernels, shards(): pl.pallas_call(functools.partial(settle_kernel, dev_count, group_count),...  30 us
    pallas_call x1, Pallas kernels, shards(): pl.pallas_call(second_kernel, out_shape=(jax.ShapeDtypeStruct((blocks, 1,...  17.2 us
    pallas_call x1, Pallas kernels, shards(): pl.pallas_call(first_kernel, out_shape=(jax.ShapeDtypeStruct((blocks, 1,...  12.8 us
    pallas_call x1, Pallas kernels, shards(): pl.pallas_call(functools.partial(close_kernel, dev_count, group_count), o...  11 us
    unnamed x23, local copies, waits for them, and re-layouts  7.71 us

profile of v2, /device:TPU:1, one launch (start us, length us, event | category | flops | bytes accessed | tf_op | source)
XLA Modules:
  0.0 125.2 jit_solution(1874117295886911261)
XLA Ops:
  0.6 0.0 copy-start.9
  0.6 0.0 copy-start.2
  0.7 0.0 copy-start.8
  0.7 0.8 dynamic_slice.23.cnt_ref
  1.5 0.1 lt.133
  1.6 0.8 fusion.4
  2.4 0.1 copy.26
  2.5 0.1 reshape.524.pos_ref
  2.5 0.8 reshape.528
  3.4 0.1 copy.27
  3.5 0.1 lt.144
  3.5 0.1 lt.145
  3.6 0.1 copy.28
  3.7 0.8 copy.29
  4.6 0.1 copy.32
  4.7 0.1 sub.99
  4.8 0.1 fusion.11
  4.9 0.0 copy-start.7
  4.9 0.1 copy.31
  5.0 0.6 select_reduce_fusion
  5.6 0.0 copy-start.1
  5.7 1.0 copy-done.1
  6.7 0.0 copy-start.4
  6.7 41.8 %deliver_blocks.1.tab_ref = bf16[40,512,128]{2,1,0:T(8,128)(2,1)S(1)} custom-call(s32[32,32]{1,0:T(8,128)S(1)} %fusion.1.pick_ref, s32[4]{0:T(128)S(1)} %compare_select_fusion.2.grp_ref, bf16[4,512,128]{2,1,0:T(8,128)(2,1)S(1)} %bitcast.17), custom_call_target="tpu_custom_call" | custom-call | tf_op jit(solution)/shard_map/deliver_blocks/pallas_call | solution.py:621
  48.5 0.0 copy-start
  48.5 2.3 %copy-done = bf16[40,512,128]{2,1,0:T(8,128)(2,1)} copy-done((bf16[40,512,128]{2,1,0:T(8,128)(2,1)}, bf16[40,512,128]{2,1,0:T(8,128)(2,1)S(1)}, u32[]{:S(2)}) %copy-start) | copy-done | bytes 5242904
  50.8 0.0 copy-done.9
  50.8 0.0 copy-done.2
  50.8 0.0 copy-done.8
  50.8 12.8 %first_pass.1 = (f32[4,1,512]{2,1,0:T(1,128)S(1)}, f32[40,1,512]{2,1,0:T(1,128)S(1)}) custom-call(s32[32]{0:T(128)S(1)} %reshape.524.pos_ref, s32[4]{0:T(128)S(1)} %dynamic_slice.23.cnt_ref, bf16[4,512,128]{2,1,0:T(8,128)(2,1)S(1)} %bitcast.23, f32[4,1,512]{2,1,0:T(1,128)S(1)} %bitcast.25, bf16[4,512,128]{2,1,0:T(8,128)(2,1)S(1)} %bitcast.18, ...), custom_call_target="tpu_custom_call" | custom-call | flops 4294967296 | bytes 6291456 | tf_op jit(solution)/shard_map/first_pass/pallas_call | solution.py:644
  63.6 0.0 copy-done.7
  63.6 0.0 copy-done.4
  63.6 0.0 copy-start.6
  63.6 0.6 copy-done.6
  64.2 30.0 %settle_first.1.first_ref = f32[40,4,128]{2,1,0:T(4,128)} custom-call(s32[32,32]{1,0:T(8,128)} %copy-done.4, s32[4]{0:T(128)} %copy-done.7, f32[40,4,128]{2,1,0:T(4,128)} %bitcast.22, f32[4,4,128]{2,1,0:T(4,128)} %bitcast.29), custom_call_target="tpu_custom_call" | custom-call | tf_op jit(solution)/shard_map/settle_first/pallas_call | solution.py:672
  94.2 0.0 copy-start.3
  94.2 0.9 copy-done.3
  95.1 17.2 %second_pass.1 = (f32[4,1,512]{2,1,0:T(1,128)}, f32[4,512,128]{2,1,0:T(8,128)}, f32[40,1,512]{2,1,0:T(1,128)S(1)}) custom-call(s32[32]{0:T(128)S(1)} %reshape.524.pos_ref, s32[4]{0:T(128)S(1)} %dynamic_slice.23.cnt_ref, bf16[4,512,128]{2,1,0:T(8,128)(2,1)S(1)} %bitcast.24, f32[4,1,512]{2,1,0:T(1,128)S(1)} %bitcast.26, ...), custom_call_target="tpu_custom_call" | custom-call | flops 8589934592 | bytes 7340032 | tf_op jit(solution)/shard_map/second_pass/pallas_call | solution.py:689
  112.3 0.0 copy-start.5
  112.3 0.6 copy-done.5
  112.9 11.0 %settle_second.1 = f32[4,4,128]{2,1,0:T(4,128)} custom-call(s32[32,32]{1,0:T(8,128)} %copy-done.4, s32[4]{0:T(128)} %copy-done.7, f32[40,4,128]{2,1,0:T(4,128)} %bitcast.21, f32[4,4,128]{2,1,0:T(4,128)} %bitcast.30, f32[40,4,128]{2,1,0:T(4,128)} %settle_first.1.first_ref), custom_call_target="tpu_custom_call" | custom-call | tf_op jit(solution)/shard_map/settle_second/pallas_call | solution.py:715
  123.9 1.3 %copy.34 = f32[2048]{0:T(1024)} copy(f32[2048]{0:T(1024)} %bitcast.31) | data formatting | bytes 16384
  (11 shorter events, 0.1 us)
Async XLA Ops:
  0.6 50.1 %copy-start.9 = (f32[2048]{0:T(1024)S(1)}, f32[2048]{0:T(1024)}, u32[]{:S(2)}) copy-start(f32[2048]{0:T(1024)} %param.8) | copy-start | bytes 24580
  0.6 50.1 %copy-start.2 = (bf16[2048,128]{1,0:T(8,128)(2,1)S(1)}, bf16[2048,128]{1,0:T(8,128)(2,1)}, u32[]{:S(2)}) copy-start(bf16[2048,128]{1,0:T(8,128)(2,1)} %param.7) | copy-start | bytes 1572868
  0.7 50.1 %copy-start.8 = (bf16[2048,128]{1,0:T(8,128)(2,1)S(1)}, bf16[2048,128]{1,0:T(8,128)(2,1)}, u32[]{:S(2)}) copy-start(bf16[2048,128]{1,0:T(8,128)(2,1)} %param.6) | copy-start | bytes 1572868
  4.9 58.7 %copy-start.7 = (s32[4]{0:T(128)}, s32[4]{0:T(128)S(1)}, u32[]{:S(2)}) copy-start(s32[4]{0:T(128)S(1)} %compare_select_fusion.2.grp_ref) | copy-start | bytes 52
  5.6 1.0 copy-start.1
  6.7 56.9 %copy-start.4 = (s32[32,32]{1,0:T(8,128)}, s32[32,32]{1,0:T(8,128)S(1)}, u32[]{:S(2)}) copy-start(s32[32,32]{1,0:T(8,128)S(1)} %fusion.1.pick_ref) | copy-start | bytes 12292
  48.5 2.3 %copy-start = (bf16[40,512,128]{2,1,0:T(8,128)(2,1)}, bf16[40,512,128]{2,1,0:T(8,128)(2,1)S(1)}, u32[]{:S(2)}) copy-start(bf16[40,512,128]{2,1,0:T(8,128)(2,1)S(1)} %deliver_blocks.1.tab_ref) | copy-start | bytes 15728644
  63.6 0.6 copy-start.6
  94.2 0.9 copy-start.3
  112.3 0.6 copy-start.5

commit v3 on v2

--- a/solution.py
+++ b/solution.py
@@ -17,7 +17,7 @@
 LOG2E = math.log2(math.e)
 ROW_LOW, ROW_HIGH, COL_LOW = 1e-6, 1e30, 1e-22
 MESH = pl.DeviceIdType.MESH
-VMEM_LIMIT = 48 * 2**20
+VMEM_LIMIT = 20 * 2**20
 
 
 RING = 4
@@ -25,12 +25,38 @@
 BRANCH = ((2, 0), (2, 1), (1, 0), (1, 1), (3, 0), (3, 1))
 
 
-def chosen_blocks(targets, counts, first, sources):
-    takers, blocks, slots = targets.shape
-    active = jnp.arange(slots, dtype=jnp.int32) < counts[:, :, None]
-    named = jnp.where(active, targets - first, -1).reshape(takers, blocks * slots, 1)
-    match = (named >= 0) & (named // blocks == sources)
-    return jnp.max(jnp.where(match, named % blocks, -1), axis=1)
+def plane_picks(targets, counts, first, sources):
+    slots = lax.broadcasted_iota(jnp.int32, targets.shape, 0)
+    named = jnp.where(slots < counts[None, :], targets - first, -1)[:, None, :]
+    source = lax.broadcasted_iota(jnp.int32, (1, sources, 1), 1)
+    return jnp.max(jnp.where((named >> 2) == source, named & 3, -1), axis=0)
+
+
+def pick_of_dev(pick_ref, taker, source):
+    first = pick_ref[source, BLK_DEV * taker]
+    for row in range(1, BLK_DEV):
+        first = jnp.maximum(first, pick_ref[source, BLK_DEV * taker + row])
+    return first
+
+
+def pick_of_group(pairs_ref, dev_count, peer, me_group, me_dev):
+    base = (peer * dev_count + me_dev) * BLK_DEV
+    mine = me_group * dev_count + me_dev
+    found = jnp.int32(-1)
+    for row in range(BLK_DEV):
+        name = pairs_ref[1, base + row]
+        found = jnp.maximum(found, jnp.where(name // BLK_DEV == mine, name % BLK_DEV, -1))
+    return found
+
+
+def table_position(pairs_ref, dev_count, myself, blk, slot):
+    name = pairs_ref[slot, myself * BLK_DEV + blk]
+    owner = name // BLK_DEV
+    group = owner // dev_count
+    away = jnp.where(
+        group == myself // dev_count, owner % dev_count, dev_count + group
+    )
+    return jnp.where(owner == myself, name % BLK_DEV, BLK_DEV + away)
 
 
 def raw_scores(left, right):
@@ -56,34 +82,6 @@
     return rows.astype(jnp.bfloat16)
 
 
-def fetch_all(pos_ref, cnt_ref, loc_ref, tab_ref, held, sems, clear):
-    @pl.loop(0, BLK_DEV * SLOTS)
-    def _(at):
-        position = pos_ref[at]
-        active = lax.rem(at, SLOTS) < cnt_ref[at // SLOTS]
-
-        @pl.when(active & (position < BLK_DEV))
-        def _():
-            pltpu.make_async_copy(loc_ref.at[position], held.at[at], sems.at[at]).start()
-
-        @pl.when(active & (position >= BLK_DEV))
-        def _():
-            pltpu.make_async_copy(tab_ref.at[position], held.at[at], sems.at[at]).start()
-
-        if clear:
-
-            @pl.when(jnp.logical_not(active))
-            def _():
-                held[at] = jnp.zeros(held.shape[1:], held.dtype)
-
-
-def await_blocks(blk, count, loc_ref, held, sems):
-    @pl.loop(0, count)
-    def _(slot):
-        at = blk * SLOTS + slot
-        pltpu.make_async_copy(loc_ref.at[0], held.at[at], sems.at[at]).wait()
-
-
 def by_width(count, work):
     @pl.when(count <= SLOTS // 2)
     def _():
@@ -101,27 +99,27 @@
 
 
 def first_kernel(
-    pos_ref, cnt_ref, src_ref, logw_ref, loc_ref, tab_ref,
+    dev_count, pairs_ref, count_ref, src_ref, logw_ref, tab_ref,
     fs_ref, part_ref,
-    held, kept, row_acc, col_max, col_sum, tab_max, tab_sum, col_tmp, sems,
+    kept, row_acc, col_sum, slow_max, slow_sum, col_tmp, slow_ref,
 ):
     factor = 1.0 / math.sqrt(EMB)
     scale = factor * LOG2E
     rows = src_ref.shape[1]
-    fetch_all(pos_ref, cnt_ref, loc_ref, tab_ref, held, sems, False)
-    tab_max[...] = jnp.full_like(tab_max, NEG_FILL)
-    tab_sum[...] = jnp.zeros_like(tab_sum)
+    myself = lax.axis_index("group") * dev_count + lax.axis_index("dev")
+    position_of = functools.partial(table_position, pairs_ref, dev_count, myself)
+    part_ref[...] = jnp.zeros_like(part_ref)
+    slow_ref[0] = jnp.int32(0)
 
     @pl.loop(0, BLK_DEV)
     def _(blk):
-        count = cnt_ref[blk]
-        await_blocks(blk, count, loc_ref, held, sems)
-        col_max[...] = jnp.zeros_like(col_max)
+        count = count_ref[myself * BLK_DEV + blk]
 
         def row_work(width):
             totals = jnp.zeros_like(row_acc)
             for slot in range(width):
-                kern = jnp.exp2(raw_scores(src_ref[blk], held[blk * SLOTS + slot]) * scale)
+                points = tab_ref[position_of(blk, slot)]
+                kern = jnp.exp2(raw_scores(src_ref[blk], points) * scale)
                 kept[slot] = kern.astype(jnp.bfloat16)
                 total = kern[:, :LANES]
                 for lane in range(1, rows // LANES):
@@ -152,17 +150,31 @@
         fine = jnp.min(jnp.where(col_fine, 1.0, 0.0), axis=0)
         fine = jnp.min(jnp.where(row_fine, fine, 0.0))
 
+        @pl.when(fine >= 0.5)
+        def _():
+            def add(width):
+                for slot in range(width):
+                    part_ref[position_of(blk, slot)] += jnp.where(slot < count, col_sum[slot], 0.0)
+
+            by_width(count, add)
+
         @pl.when(fine < 0.5)
         def _():
+            @pl.when(slow_ref[0] == 0)
+            def _():
+                slow_ref[0] = jnp.int32(1)
+                slow_max[...] = jnp.full_like(slow_max, NEG_FILL)
+                slow_sum[...] = jnp.zeros_like(slow_sum)
+
             row_acc[...] = jnp.full_like(row_acc, NEG_FILL)
             col_tmp[...] = jnp.zeros_like(col_tmp)
 
             @pl.loop(0, count)
             def _(slot):
-                at = blk * SLOTS + slot
+                points = tab_ref[position_of(blk, slot)]
                 for part in range(rows // LANES):
                     span = pl.ds(part * LANES, LANES)
-                    scores = raw_scores(src_ref[blk, span, :], held[at]) * factor
+                    scores = raw_scores(src_ref[blk, span, :], points) * factor
                     old = row_acc[span, :]
                     new = jnp.maximum(old, jnp.max(scores, axis=1, keepdims=True))
                     here = jnp.sum(jnp.exp(scores - new[:, 0:1]), axis=1, keepdims=True)
@@ -175,63 +187,63 @@
 
             @pl.loop(0, count)
             def _(slot):
-                at = blk * SLOTS + slot
+                position = position_of(blk, slot)
+                points = tab_ref[position]
                 high = jnp.full((1, rows), NEG_FILL, jnp.float32)
                 total = jnp.zeros((1, rows), jnp.float32)
                 for part in range(rows // LANES):
                     span = pl.ds(part * LANES, LANES)
-                    scores = raw_scores(src_ref[blk, span, :], held[at]) * factor
+                    scores = raw_scores(src_ref[blk, span, :], points) * factor
                     scores = scores + row_acc[span, 0:1]
                     new = jnp.maximum(high, jnp.max(scores, axis=0, keepdims=True))
                     total = total * jnp.exp(high - new) + jnp.sum(
                         jnp.exp(scores - new), axis=0, keepdims=True
                     )
                     high = new
-                col_max[slot] = high
-                col_sum[slot] = total
-
-        @pl.loop(0, count)
-        def _(slot):
-            position = pos_ref[blk * SLOTS + slot]
-            old = tab_max[position]
-            high = col_max[slot]
-            new = jnp.maximum(old, high)
-            tab_sum[position] = tab_sum[position] * jnp.exp(old - new) + col_sum[slot] * jnp.exp(
-                high - new
-            )
-            tab_max[position] = new
-
-    sums = tab_sum[...]
-    used = sums > 0.0
-    part_ref[...] = jnp.where(
-        used, tab_max[...] + jnp.log(jnp.where(used, sums, 1.0)), NEG_FILL
-    )
+                old = slow_max[position]
+                new = jnp.maximum(old, high)
+                slow_sum[position] = slow_sum[position] * jnp.exp(old - new) + total * jnp.exp(
+                    high - new
+                )
+                slow_max[position] = new
+
+    sums = part_ref[...]
+    lse = jnp.where(sums > 0.0, jnp.log(jnp.where(sums > 0.0, sums, 1.0)), NEG_FILL)
+    part_ref[...] = lse
+
+    @pl.when(slow_ref[0] == 1)
+    def _():
+        fast, sums = part_ref[...], slow_sum[...]
+        slow = slow_max[...] + jnp.log(jnp.where(sums > 0.0, sums, 1.0))
+        slow = jnp.where(sums > 0.0, slow, NEG_FILL)
+        high = jnp.maximum(fast, slow)
+        part_ref[...] = high + jnp.log(jnp.exp(fast - high) + jnp.exp(slow - high))
 
 
 def second_kernel(
-    pos_ref, cnt_ref, src_ref, logw_ref, fs_ref, dual_ref, loc_ref, tab_ref,
+    dev_count, pairs_ref, count_ref, src_ref, logw_ref, fs_ref, dual_ref, tab_ref,
     pot_ref, map_ref, sum_ref,
-    held, kept, fs_col, acc, sems,
+    kept, fs_col, acc,
 ):
     scale = LOG2E / math.sqrt(EMB)
     rows = src_ref.shape[1]
-    fetch_all(pos_ref, cnt_ref, loc_ref, tab_ref, held, sems, True)
+    myself = lax.axis_index("group") * dev_count + lax.axis_index("dev")
+    position_of = functools.partial(table_position, pairs_ref, dev_count, myself)
     sum_ref[...] = jnp.zeros_like(sum_ref)
     ones = jnp.ones((rows, LANES), jnp.bfloat16)
 
     @pl.loop(0, BLK_DEV)
     def _(blk):
-        count = cnt_ref[blk]
-        await_blocks(blk, count, loc_ref, held, sems)
+        count = count_ref[myself * BLK_DEV + blk]
         first_source = fs_ref[blk]
         fs_col[...] = as_columns(first_source * LOG2E)
         acc[...] = jnp.zeros_like(acc)
 
         def row_work(width):
             for slot in range(width):
-                at = blk * SLOTS + slot
-                dual = jnp.where(slot < count, dual_ref[pos_ref[at]] * LOG2E, NEG_FILL)
-                points = held[at]
+                position = position_of(blk, slot)
+                dual = jnp.where(slot < count, dual_ref[position] * LOG2E, NEG_FILL)
+                points = tab_ref[position]
                 beside = jnp.concatenate([points, ones], axis=1)
                 for part in range(rows // LANES):
                     span = pl.ds(part * LANES, LANES)
@@ -252,17 +264,16 @@
 
         def column_work(width):
             for slot in range(width):
-                position = pos_ref[blk * SLOTS + slot]
                 here = column_sums(weights, kept, slot)
-                sum_ref[position] += jnp.where(slot < count, here, 0.0)
+                sum_ref[position_of(blk, slot)] += jnp.where(slot < count, here, 0.0)
 
         by_width(count, column_work)
 
 
 def deliver_kernel(
-    dev_count, group_count, pick_ref, grp_ref, tgt_ref, tab_ref,
+    dev_count, group_count, pick_ref, pairs_ref, tgt_ref, tab_ref,
     prev_buf, next_buf, far_buf, relay_up, relay_down, stage,
-    trunk_send, trunk_recv, stage_send, tab_recv, relay_recv, fwd_send, grp_recv,
+    trunk_send, trunk_recv, stage_send, tab_recv, relay_recv, fwd_send, grp_recv, own_sem,
 ):
     me_group, me_dev = lax.axis_index("group"), lax.axis_index("dev")
     core = lax.rem(me_dev, 2)
@@ -322,7 +333,7 @@
         for n, (across, to_core) in enumerate(BRANCH + ((0, 1 - core),)):
             taker = device(0, across, to_core)
             at = k * (len(BRANCH) + 1) + n
-            stage[at] = buf[jnp.maximum(pick_ref[taker, source], 0)]
+            stage[at] = buf[jnp.maximum(pick_of_dev(pick_ref, taker, source), 0)]
             if across == 2:
                 relay, over = ((relay_up, 1), (relay_down, 3))[to_core]
                 which = relay_recv.at[to_core * RING + k]
@@ -341,7 +352,7 @@
             sent.append(copy)
         if k > 0:
             at = RING * (len(BRANCH) + 1) + group_count - 1 + k - 1
-            stage[at] = buf[jnp.maximum(pick_ref[me_dev, source], 0)]
+            stage[at] = buf[jnp.maximum(pick_of_dev(pick_ref, me_dev, source), 0)]
             pltpu.make_async_copy(
                 stage.at[at], tab_ref.at[BLK_DEV + source], tab_recv.at[source]
             ).start()
@@ -364,11 +375,14 @@
             sent.append(copy)
 
     branch(0, tgt_ref)
+    own = pltpu.make_async_copy(tgt_ref, tab_ref.at[pl.ds(0, BLK_DEV)], own_sem.at[0])
+    own.start()
     from_groups = []
     for step in range(1, group_count):
         peer = lax.rem(me_group + step, group_count)
         at = RING * (len(BRANCH) + 1) + step - 1
-        stage[at] = tgt_ref[jnp.maximum(grp_ref[peer], 0)]
+        pick = pick_of_group(pairs_ref, dev_count, peer, me_group, me_dev)
+        stage[at] = tgt_ref[jnp.maximum(pick, 0)]
         copy = send(
             stage.at[at],
             tab_ref.at[BLK_DEV + dev_count + me_group],
@@ -404,6 +418,7 @@
         ).wait_recv()
     for copy in from_groups:
         copy.wait_recv()
+    own.wait()
 
 
 def greet(dev_count, group_count, me_dev, me_group):
@@ -469,105 +484,74 @@
     lax.fori_loop(1, group_count, wait(to_group), 0)
 
 
-def picker(pick_ref, grp_ref, dev_count, me_dev):
-    def pick_of(e):
-        of_dev = pick_ref[jnp.minimum(e, dev_count - 1), me_dev]
-        return jnp.where(e < dev_count, of_dev, grp_ref[jnp.maximum(e - dev_count, 0)])
-
-    return pick_of
+def picks_of_peers(pick_ref, pairs_ref, dev_count, group_count, me_group, me_dev):
+    return [
+        jnp.where(me_dev == e, -1, pick_of_dev(pick_ref, e, me_dev)) for e in range(dev_count)
+    ] + [
+        jnp.where(me_group == e, -1, pick_of_group(pairs_ref, dev_count, e, me_group, me_dev))
+        for e in range(group_count)
+    ]
 
 
 def settle_kernel(
-    dev_count, group_count, pick_ref, grp_ref, part_ref, logw_ref, dual_ref,
+    dev_count, group_count, pick_ref, pairs_ref, part_ref, logw_ref, dual_ref,
     inbox, outbox, send_a, recv_a, send_b, recv_b,
 ):
     me_group, me_dev = lax.axis_index("group"), lax.axis_index("dev")
     blocks = BLK_DEV
-    peers = dev_count + group_count
     empty = jnp.full(inbox.shape[1:], NEG_FILL, jnp.float32)
     greet(dev_count, group_count, me_dev, me_group)
     inbox[me_dev] = empty
     inbox[dev_count + me_group] = empty
+    picks = picks_of_peers(pick_ref, pairs_ref, dev_count, group_count, me_group, me_dev)
     exchange(
         part_ref, blocks, inbox, 0, send_a, recv_a, dev_count, group_count, me_dev, me_group
     )
-    own = [part_ref[q] for q in range(blocks)]
-
-    pick_of = picker(pick_ref, grp_ref, dev_count, me_dev)
-
-    def highest(e, carry):
-        pick, here = pick_of(e), inbox[e]
-        return tuple(
-            jnp.maximum(high, jnp.where(pick == q, here, NEG_FILL)) for q, high in enumerate(carry)
-        )
-
-    highs = lax.fori_loop(0, peers, highest, tuple(own))
-
-    def summed(e, carry):
-        pick, here = pick_of(e), inbox[e]
-        return tuple(
-            total + jnp.exp(jnp.where(pick == q, here, NEG_FILL) - highs[q])
-            for q, total in enumerate(carry)
-        )
-
-    totals = lax.fori_loop(
-        0, peers, summed, tuple(jnp.exp(o - h) for o, h in zip(own, highs))
-    )
-    duals = [
-        logw_ref[q] - (highs[q] + jnp.log(totals[q])) for q in range(blocks)
-    ]
+    duals = []
     for q in range(blocks):
+        terms = [part_ref[q]] + [
+            jnp.where(pick == q, inbox[e], NEG_FILL) for e, pick in enumerate(picks)
+        ]
+        high = functools.reduce(jnp.maximum, terms)
+        total = sum(jnp.exp(term - high) for term in terms)
+        duals.append(logw_ref[q] - (high + jnp.log(total)))
         dual_ref[q] = duals[q]
-
-    def fill(e, carry):
-        pick = pick_of(e)
-        chosen = jnp.zeros_like(duals[0])
-        for q in range(blocks):
+    for e, pick in enumerate(picks):
+        chosen = duals[0]
+        for q in range(1, blocks):
             chosen = jnp.where(pick == q, duals[q], chosen)
         outbox[e] = chosen
-        return carry
-
-    lax.fori_loop(0, peers, fill, 0)
-    dual_ref[blocks + me_dev] = jnp.zeros_like(duals[0])
-    dual_ref[blocks + dev_count + me_group] = jnp.zeros_like(duals[0])
+    dual_ref[blocks + me_dev] = jnp.zeros_like(empty)
+    dual_ref[blocks + dev_count + me_group] = jnp.zeros_like(empty)
     exchange(
         outbox, 0, dual_ref, blocks, send_b, recv_b, dev_count, group_count, me_dev, me_group
     )
 
 
 def close_kernel(
-    dev_count, group_count, pick_ref, grp_ref, sum_ref, logw_ref, first_ref, pot_ref,
+    dev_count, group_count, pick_ref, pairs_ref, sum_ref, logw_ref, first_ref, pot_ref,
     inbox, send_a, recv_a,
 ):
     me_group, me_dev = lax.axis_index("group"), lax.axis_index("dev")
     blocks = BLK_DEV
-    peers = dev_count + group_count
     greet(dev_count, group_count, me_dev, me_group)
     inbox[me_dev] = jnp.zeros(inbox.shape[1:], jnp.float32)
     inbox[dev_count + me_group] = jnp.zeros(inbox.shape[1:], jnp.float32)
+    picks = picks_of_peers(pick_ref, pairs_ref, dev_count, group_count, me_group, me_dev)
     exchange(
         sum_ref, blocks, inbox, 0, send_a, recv_a, dev_count, group_count, me_dev, me_group
     )
-
-    pick_of = picker(pick_ref, grp_ref, dev_count, me_dev)
-
-    def summed(e, carry):
-        pick, here = pick_of(e), inbox[e]
-        return tuple(
-            total + jnp.where(pick == q, here, 0.0) for q, total in enumerate(carry)
-        )
-
-    totals = lax.fori_loop(0, peers, summed, tuple(sum_ref[q] for q in range(blocks)))
     for q in range(blocks):
-        pot_ref[q] = logw_ref[q] - jnp.log(totals[q]) + first_ref[q]
+        total = sum_ref[q]
+        for e, pick in enumerate(picks):
+            total = total + jnp.where(pick == q, inbox[e], 0.0)
+        pot_ref[q] = logw_ref[q] - jnp.log(total) + first_ref[q]
 
 
 def shards(source_points, target_points, source_logw, target_logw, pair_targets, pair_count):
     group_count = lax.axis_size("group")
     dev_count = lax.axis_size("dev")
     group_idx = lax.axis_index("group")
-    dev_idx = lax.axis_index("dev")
-    myself = group_idx * dev_count + dev_idx
     blocks, rows, slots = BLK_DEV, BLOCK, SLOTS
     table = blocks + dev_count + group_count
     peers = dev_count + group_count
@@ -576,44 +560,20 @@
     log_src = source_logw.reshape(blocks, 1, rows)
     log_tgt = target_logw.reshape(blocks, rows // LANES, LANES)
 
-    own_targets = lax.dynamic_slice_in_dim(pair_targets, myself * blocks, blocks, 0)
-    own_counts = lax.dynamic_slice_in_dim(pair_count, myself * blocks, blocks, 0)
-    owners = own_targets // blocks
-    position = jnp.where(
-        owners == myself,
-        own_targets % blocks,
-        jnp.where(
-            owners // dev_count == group_idx,
-            blocks + owners % dev_count,
-            blocks + dev_count + owners // dev_count,
-        ),
-    ).reshape(blocks * slots)
-    everything = pair_targets.reshape(group_count, dev_count, blocks, slots)
-    counts_all = pair_count.reshape(group_count, dev_count, blocks)
-    pick = chosen_blocks(
-        lax.dynamic_index_in_dim(everything, group_idx, 0, keepdims=False),
-        lax.dynamic_index_in_dim(counts_all, group_idx, 0, keepdims=False),
-        group_idx * dev_count * blocks,
-        jnp.arange(dev_count, dtype=jnp.int32),
-    )
-    pick_grp = chosen_blocks(
-        lax.dynamic_index_in_dim(everything, dev_idx, 1, keepdims=False),
-        lax.dynamic_index_in_dim(counts_all, dev_idx, 1, keepdims=False),
-        myself * blocks,
-        jnp.zeros((1,), jnp.int32),
-    )[:, 0]
-    pick = jnp.where(
-        jnp.arange(dev_count)[:, None] == jnp.arange(dev_count)[None, :], -1, pick
-    )
-    pick_grp = jnp.where(jnp.arange(group_count) == group_idx, -1, pick_grp)
+    plane = dev_count * blocks
+    named = pair_targets.T
+    pick = plane_picks(
+        lax.dynamic_slice_in_dim(named, group_idx * plane, plane, 1),
+        lax.dynamic_slice_in_dim(pair_count, group_idx * plane, plane, 0),
+        group_idx * plane,
+        dev_count,
+    )
 
     smem = pl.BlockSpec(memory_space=pltpu.SMEM)
     vmem = pl.BlockSpec(memory_space=pltpu.VMEM)
     anywhere = pl.BlockSpec(memory_space=pl.ANY)
     f32 = jnp.float32
-    held = pltpu.VMEM((blocks * slots, rows, EMB), jnp.bfloat16)
     kept = pltpu.VMEM((slots, rows, rows), jnp.bfloat16)
-    copy_sems = pltpu.SemaphoreType.DMA((blocks * slots,))
     pairs = blocks * slots
     dma = pltpu.SemaphoreType.DMA
     block = (rows, EMB)
@@ -634,38 +594,37 @@
             dma((2 * RING,)),
             dma((2 * RING,)),
             dma((group_count,)),
+            dma((1,)),
         ],
         compiler_params=pltpu.CompilerParams(
             collective_id=2, has_side_effects=True, vmem_limit_bytes=VMEM_LIMIT
         ),
         name="deliver_blocks",
-    )(pick, pick_grp, targets)
+    )(pick, named, targets)
 
     first_source, part = pl.pallas_call(
-        first_kernel,
+        functools.partial(first_kernel, dev_count),
         out_shape=(
             jax.ShapeDtypeStruct((blocks, 1, rows), f32),
             jax.ShapeDtypeStruct((table, 1, rows), f32),
         ),
-        in_specs=[smem, smem, vmem, vmem, anywhere, anywhere],
+        in_specs=[smem, smem, vmem, vmem, vmem],
         out_specs=(vmem, vmem),
         scratch_shapes=[
-            held,
             kept,
             pltpu.VMEM((rows, LANES), f32),
-            pltpu.VMEM((slots, 1, rows), f32),
             pltpu.VMEM((slots, 1, rows), f32),
             pltpu.VMEM((table, 1, rows), f32),
             pltpu.VMEM((table, 1, rows), f32),
             pltpu.VMEM((rows, LANES), f32),
-            copy_sems,
+            pltpu.SMEM((1,), jnp.int32),
         ],
         compiler_params=pltpu.CompilerParams(vmem_limit_bytes=VMEM_LIMIT),
         cost_estimate=pl.CostEstimate(
             flops=4 * pairs * rows * rows * EMB, bytes_accessed=6 * 2**20, transcendentals=pairs * rows * rows
         ),
         name="first_pass",
-    )(position, own_counts, sources, log_src, targets, delivered)
+    )(named, pair_count, sources, log_src, delivered)
 
     small = (rows // LANES, LANES)
     sems = pltpu.SemaphoreType.DMA((peers,))
@@ -682,25 +641,25 @@
             sems,
             sems,
         ],
-        compiler_params=pltpu.CompilerParams(collective_id=0, has_side_effects=True),
+        compiler_params=pltpu.CompilerParams(
+            collective_id=0, has_side_effects=True, vmem_limit_bytes=4 * 2**20
+        ),
         name="settle_first",
-    )(pick, pick_grp, part.reshape(table, *small), log_tgt)
+    )(pick, named, part.reshape(table, *small), log_tgt)
 
     potential, mapped, col_sums = pl.pallas_call(
-        second_kernel,
+        functools.partial(second_kernel, dev_count),
         out_shape=(
             jax.ShapeDtypeStruct((blocks, 1, rows), f32),
             jax.ShapeDtypeStruct((blocks, rows, EMB), f32),
             jax.ShapeDtypeStruct((table, 1, rows), f32),
         ),
-        in_specs=[smem, smem, vmem, vmem, vmem, vmem, anywhere, anywhere],
+        in_specs=[smem, smem, vmem, vmem, vmem, vmem, vmem],
         out_specs=(vmem, vmem, vmem),
         scratch_shapes=[
-            held,
             kept,
             pltpu.VMEM((rows, LANES), f32),
             pltpu.VMEM((rows, 2 * LANES), f32),
-            copy_sems,
         ],
         compiler_params=pltpu.CompilerParams(vmem_limit_bytes=VMEM_LIMIT),
         cost_estimate=pl.CostEstimate(
@@ -708,8 +667,8 @@
         ),
         name="second_pass",
     )(
-        position, own_counts, sources, log_src, first_source,
-        dual.reshape(table, 1, rows), targets, delivered,
+        named, pair_count, sources, log_src, first_source,
+        dual.reshape(table, 1, rows), delivered,
     )
 
     target_potential = pl.pallas_call(
@@ -718,9 +677,11 @@
         in_specs=[smem, smem, vmem, vmem, vmem],
         out_specs=vmem,
         scratch_shapes=[pltpu.VMEM((peers, *small), f32), sems, sems],
-        compiler_params=pltpu.CompilerParams(collective_id=1, has_side_effects=True),
+        compiler_params=pltpu.CompilerParams(
+            collective_id=1, has_side_effects=True, vmem_limit_bytes=4 * 2**20
+        ),
         name="settle_second",
-    )(pick, pick_grp, col_sums.reshape(table, *small), log_tgt, dual)
+    )(pick, named, col_sums.reshape(table, *small), log_tgt, dual)
     return (
         potential.reshape(blocks * rows),
         target_potential.reshape(blocks * rows),

time: 126 us -> 113 us (0.90)
  local copies, waits for them, and re-layouts: 10.1 us -> 3.18 us
  Pallas kernels: 113 us -> 108 us
    pallas_call x2, Pallas kernels: 30 us -> 18 us  [the longest x1 10 us: shards(): pl.pallas_call(functools.partial(second_kernel, dev_count), out_shape=(ja...]
    unnamed x23 -> x13, local copies, waits for them, and re-layouts: 7.71 us -> 2.37 us
    pallas_call x1, Pallas kernels: 11 us -> 15.6 us  [shards(): pl.pallas_call(functools.partial(close_kernel, dev_count, group_count), o...]
    pallas_call x1, Pallas kernels: 30 us -> 32.9 us  [shards(): pl.pallas_call(functools.partial(settle_kernel, dev_count, group_count),...]
where the time goes in v3:
time: 113 us
  Pallas kernels  108 us (96%)
  local copies, waits for them, and re-layouts  3.18 us (3%)
    pallas_call x1, Pallas kernels, shards(): pl.pallas_call(functools.partial(deliver_kernel, dev_count, group_count),...  42 us
    pallas_call x1, Pallas kernels, shards(): pl.pallas_call(functools.partial(settle_kernel, dev_count, group_count),...  32.9 us
    pallas_call x1, Pallas kernels, shards(): pl.pallas_call(functools.partial(close_kernel, dev_count, group_count), o...  15.6 us
    pallas_call x1, Pallas kernels, shards(): pl.pallas_call(functools.partial(second_kernel, dev_count), out_shape=(ja...  10 us
    pallas_call x1, Pallas kernels, shards(): pl.pallas_call(functools.partial(first_kernel, dev_count), out_shape=(jax...  7.94 us
    unnamed x13, local copies, waits for them, and re-layouts  2.37 us

profile of v3, /device:TPU:1, one launch (start us, length us, event | category | flops | bytes accessed | tf_op | source)
XLA Modules:
  0.0 113.1 jit_solution(14884846629086908070)
XLA Ops:
  0.6 0.0 copy-start.5
  0.6 0.0 copy-start.4
  0.7 0.8 dynamic_slice.6
  1.5 0.7 fusion.1
  2.2 0.0 copy-start
  2.2 1.0 copy-done
  3.2 0.0 copy-start.1
  3.2 0.7 copy-done.1
  3.9 0.0 copy-start.3
  3.9 42.0 %deliver_blocks.1.tab_ref = bf16[40,512,128]{2,1,0:T(8,128)(2,1)S(1)} custom-call(s32[32,128]{1,0:T(8,128)S(1)} %select_reduce_fusion.pick_ref, s32[8,512]{1,0:T(8,128)S(1)} %bitcast.19, bf16[4,512,128]{2,1,0:T(8,128)(2,1)S(1)} %bitcast.17), custom_call_target="tpu_custom_call" | custom-call | tf_op jit(solution)/shard_map/deliver_blocks/pallas_call | solution.py:581
  46.0 0.0 copy-done.5
  46.0 0.0 copy-done.4
  46.0 0.0 copy-done.3
  46.0 0.0 copy-start.2
  46.0 7.9 %first_pass.1 = (f32[4,1,512]{2,1,0:T(1,128)S(1)}, f32[40,1,512]{2,1,0:T(1,128)S(1)}) custom-call(s32[8,512]{1,0:T(8,128)S(1)} %bitcast.20, s32[512]{0:T(512)S(1)} %copy-done.5, bf16[4,512,128]{2,1,0:T(8,128)(2,1)S(1)} %bitcast.29, f32[4,1,512]{2,1,0:T(1,128)S(1)} %bitcast.31, bf16[40,512,128]{2,1,0:T(8,128)(2,1)S(1)} %deliver_blocks.1.tab_ref), custom_call_target="tpu_custom_call" | custom-call | flops 4294967296 | bytes 6291456 | tf_op jit(solution)/shard_map/first_pass/pallas_call | solution.py:605
  54.0 0.0 copy-done.2
  54.0 32.9 %settle_first.1.first_ref = f32[40,4,128]{2,1,0:T(4,128)S(1)} custom-call(s32[32,128]{1,0:T(8,128)S(1)} %select_reduce_fusion.pick_ref, s32[8,512]{1,0:T(8,128)S(1)} %bitcast.21, f32[40,4,128]{2,1,0:T(4,128)S(1)} %bitcast.24, f32[4,4,128]{2,1,0:T(4,128)S(1)} %bitcast.26), custom_call_target="tpu_custom_call" | custom-call | tf_op jit(solution)/shard_map/settle_first/pallas_call | solution.py:631
  86.9 10.0 %second_pass.1 = (f32[4,1,512]{2,1,0:T(1,128)}, f32[4,512,128]{2,1,0:T(8,128)}, f32[40,1,512]{2,1,0:T(1,128)S(1)}) custom-call(s32[8,512]{1,0:T(8,128)S(1)} %bitcast.22, s32[512]{0:T(512)S(1)} %copy-done.5, bf16[4,512,128]{2,1,0:T(8,128)(2,1)S(1)} %bitcast.30, f32[4,1,512]{2,1,0:T(1,128)S(1)} %bitcast.32, f32[4,1,512]{2,1,0:T(1,128)S(1)} %get-tuple-element.8.fs_ref, ...), custom_call_target="tpu_custom_call" | custom-call | flops 8589934592 | bytes 7340032 | tf_op jit(solution)/shard_map/second_pass/pallas_call | solution.py:650
  96.9 15.6 %settle_second.1 = f32[4,4,128]{2,1,0:T(4,128)S(1)} custom-call(s32[32,128]{1,0:T(8,128)S(1)} %select_reduce_fusion.pick_ref, s32[8,512]{1,0:T(8,128)S(1)} %bitcast.23, f32[40,4,128]{2,1,0:T(4,128)S(1)} %bitcast.25, f32[4,4,128]{2,1,0:T(4,128)S(1)} %bitcast.27, f32[40,4,128]{2,1,0:T(4,128)S(1)} %settle_first.1.first_ref), custom_call_target="tpu_custom_call" | custom-call | tf_op jit(solution)/shard_map/settle_second/pallas_call | solution.py:674
  112.5 0.6 copy.10
  (1 shorter events, 0.0 us)
Async XLA Ops:
  0.6 45.4 %copy-start.5 = (s32[512]{0:T(512)S(1)}, s32[512]{0:T(512)}, u32[]{:S(2)}) copy-start(s32[512]{0:T(512)} %count_ref.3) | copy-start | bytes 6148
  0.6 45.4 %copy-start.4 = (f32[2048]{0:T(1024)S(1)}, f32[2048]{0:T(1024)}, u32[]{:S(2)}) copy-start(f32[2048]{0:T(1024)} %param.8) | copy-start | bytes 24580
  2.2 1.0 copy-start
  3.2 0.7 copy-start.1
  3.9 42.1 %copy-start.3 = (bf16[2048,128]{1,0:T(8,128)(2,1)S(1)}, bf16[2048,128]{1,0:T(8,128)(2,1)}, u32[]{:S(2)}) copy-start(bf16[2048,128]{1,0:T(8,128)(2,1)} %param.6) | copy-start | bytes 1572868
  46.0 8.0 %copy-start.2 = (f32[2048]{0:T(1024)S(1)}, f32[2048]{0:T(1024)}, u32[]{:S(2)}) copy-start(f32[2048]{0:T(1024)} %param.9) | copy-start | bytes 24580

commit v4 on v3

--- a/solution.py
+++ b/solution.py
@@ -18,6 +18,7 @@
 ROW_LOW, ROW_HIGH, COL_LOW = 1e-6, 1e30, 1e-22
 MESH = pl.DeviceIdType.MESH
 VMEM_LIMIT = 20 * 2**20
+PAIR_LIMIT = 36 * 2**20
 
 
 RING = 4
@@ -92,82 +93,88 @@
         work(SLOTS)
 
 
-def column_sums(weights, kept, slot):
+def column_sums(weights, kernel):
     return jnp.sum(
-        jnp.dot(weights, kept[slot], preferred_element_type=jnp.float32), axis=0, keepdims=True
+        jnp.dot(weights, kernel, preferred_element_type=jnp.float32), axis=0, keepdims=True
     )
 
 
 def first_kernel(
     dev_count, pairs_ref, count_ref, src_ref, logw_ref, tab_ref,
     fs_ref, part_ref,
-    kept, row_acc, col_sum, slow_max, slow_sum, col_tmp, slow_ref,
+    kept, row_acc, wts, fine_ref, col_max, col_total,
 ):
     factor = 1.0 / math.sqrt(EMB)
     scale = factor * LOG2E
     rows = src_ref.shape[1]
     myself = lax.axis_index("group") * dev_count + lax.axis_index("dev")
     position_of = functools.partial(table_position, pairs_ref, dev_count, myself)
-    part_ref[...] = jnp.zeros_like(part_ref)
-    slow_ref[0] = jnp.int32(0)
 
     @pl.loop(0, BLK_DEV)
     def _(blk):
         count = count_ref[myself * BLK_DEV + blk]
 
         def row_work(width):
-            totals = jnp.zeros_like(row_acc)
+            totals = jnp.zeros((rows, LANES), jnp.float32)
             for slot in range(width):
                 points = tab_ref[position_of(blk, slot)]
                 kern = jnp.exp2(raw_scores(src_ref[blk], points) * scale)
-                kept[slot] = kern.astype(jnp.bfloat16)
+                kept[blk * SLOTS + slot] = kern.astype(jnp.bfloat16)
                 total = kern[:, :LANES]
                 for lane in range(1, rows // LANES):
                     total = total + kern[:, lane * LANES : (lane + 1) * LANES]
                 totals = totals + jnp.where(slot < count, total, 0.0)
-            row_acc[...] = totals
+            row_acc[pl.ds(blk * rows, rows), :] = totals
 
         by_width(count, row_work)
-        row_sum = lax.dot_general(
-            jnp.ones((8, LANES), jnp.float32),
-            row_acc[...],
-            (((1,), (1,)), ((), ())),
-            precision=lax.Precision.HIGHEST,
-            preferred_element_type=jnp.float32,
-        )[0:1]
-        logw = logw_ref[blk]
-        fs_ref[blk] = logw - jnp.log(row_sum)
-        weights = weight_rows(jnp.exp(logw) / row_sum)
+
+    row_sum = lax.dot_general(
+        jnp.ones((8, LANES), jnp.float32),
+        row_acc[...],
+        (((1,), (1,)), ((), ())),
+        precision=lax.Precision.HIGHEST,
+        preferred_element_type=jnp.float32,
+    )[0:1]
+    logw = logw_ref[...]
+    fs_ref[...] = logw - jnp.log(row_sum)
+    weights = weight_rows(jnp.exp(logw) / row_sum)
+    row_fine = jnp.where((row_sum >= ROW_LOW) & (row_sum <= ROW_HIGH), 1.0, 0.0)
+    fine = jnp.ones((1, rows), jnp.float32)
+    for blk in range(BLK_DEV):
+        span = slice(blk * rows, (blk + 1) * rows)
+        wts[blk] = weights[:, span]
+        fine = jnp.minimum(fine, row_fine[:, span])
+    fine_ref[...] = fine
+    part_ref[...] = jnp.zeros_like(part_ref)
+
+    @pl.loop(0, BLK_DEV)
+    def _(blk):
+        count = count_ref[myself * BLK_DEV + blk]
 
         def column_work(width):
+            fine = fine_ref[...]
             for slot in range(width):
-                col_sum[slot] = column_sums(weights, kept, slot)
+                here = column_sums(wts[blk], kept[blk * SLOTS + slot])
+                part_ref[position_of(blk, slot)] += jnp.where(slot < count, here, 0.0)
+                fine = jnp.minimum(
+                    fine, jnp.where((here >= COL_LOW) | (slot >= count), 1.0, 0.0)
+                )
+            fine_ref[...] = fine
 
         by_width(count, column_work)
-        row_fine = (row_sum >= ROW_LOW) & (row_sum <= ROW_HIGH)
-        slot_at = lax.broadcasted_iota(jnp.int32, col_sum.shape, 0)
-        col_fine = (slot_at >= count) | (col_sum[...] >= COL_LOW)
-        fine = jnp.min(jnp.where(col_fine, 1.0, 0.0), axis=0)
-        fine = jnp.min(jnp.where(row_fine, fine, 0.0))
-
-        @pl.when(fine >= 0.5)
-        def _():
-            def add(width):
-                for slot in range(width):
-                    part_ref[position_of(blk, slot)] += jnp.where(slot < count, col_sum[slot], 0.0)
-
-            by_width(count, add)
-
-        @pl.when(fine < 0.5)
-        def _():
-            @pl.when(slow_ref[0] == 0)
-            def _():
-                slow_ref[0] = jnp.int32(1)
-                slow_max[...] = jnp.full_like(slow_max, NEG_FILL)
-                slow_sum[...] = jnp.zeros_like(slow_sum)
-
-            row_acc[...] = jnp.full_like(row_acc, NEG_FILL)
-            col_tmp[...] = jnp.zeros_like(col_tmp)
+
+    sums = part_ref[...]
+    part_ref[...] = jnp.where(sums > 0.0, jnp.log(jnp.where(sums > 0.0, sums, 1.0)), NEG_FILL)
+
+    @pl.when(jnp.min(fine_ref[...]) < 0.5)
+    def _():
+        part_ref[...] = jnp.full_like(part_ref, NEG_FILL)
+
+        @pl.loop(0, BLK_DEV)
+        def _(blk):
+            count = count_ref[myself * BLK_DEV + blk]
+            col_max[...] = jnp.full_like(col_max, NEG_FILL)
+            col_total[...] = jnp.zeros_like(col_total)
 
             @pl.loop(0, count)
             def _(slot):
@@ -175,99 +182,39 @@
                 for part in range(rows // LANES):
                     span = pl.ds(part * LANES, LANES)
                     scores = raw_scores(src_ref[blk, span, :], points) * factor
-                    old = row_acc[span, :]
+                    old = col_max[span, :]
                     new = jnp.maximum(old, jnp.max(scores, axis=1, keepdims=True))
                     here = jnp.sum(jnp.exp(scores - new[:, 0:1]), axis=1, keepdims=True)
-                    col_tmp[span, :] = col_tmp[span, :] * jnp.exp(old - new) + here
-                    row_acc[span, :] = new
-
-            source = as_columns(logw_ref[blk]) - (row_acc[...] + jnp.log(col_tmp[...]))
-            row_acc[...] = source
-            fs_ref[blk] = as_row(source)
+                    col_total[span, :] = col_total[span, :] * jnp.exp(old - new) + here
+                    col_max[span, :] = new
+
+            lse = col_max[...] + jnp.log(col_total[...])
+            row_acc[pl.ds(blk * rows, rows), :] = lse
 
             @pl.loop(0, count)
             def _(slot):
                 position = position_of(blk, slot)
                 points = tab_ref[position]
+                logw_col = as_columns(logw_ref[:, pl.ds(pl.multiple_of(blk * rows, rows), rows)])
+                source = logw_col - row_acc[pl.ds(blk * rows, rows), :]
+                col_max[...] = source
                 high = jnp.full((1, rows), NEG_FILL, jnp.float32)
                 total = jnp.zeros((1, rows), jnp.float32)
                 for part in range(rows // LANES):
                     span = pl.ds(part * LANES, LANES)
                     scores = raw_scores(src_ref[blk, span, :], points) * factor
-                    scores = scores + row_acc[span, 0:1]
+                    scores = scores + col_max[span, 0:1]
                     new = jnp.maximum(high, jnp.max(scores, axis=0, keepdims=True))
                     total = total * jnp.exp(high - new) + jnp.sum(
                         jnp.exp(scores - new), axis=0, keepdims=True
                     )
                     high = new
-                old = slow_max[position]
-                new = jnp.maximum(old, high)
-                slow_sum[position] = slow_sum[position] * jnp.exp(old - new) + total * jnp.exp(
-                    high - new
-                )
-                slow_max[position] = new
-
-    sums = part_ref[...]
-    lse = jnp.where(sums > 0.0, jnp.log(jnp.where(sums > 0.0, sums, 1.0)), NEG_FILL)
-    part_ref[...] = lse
-
-    @pl.when(slow_ref[0] == 1)
-    def _():
-        fast, sums = part_ref[...], slow_sum[...]
-        slow = slow_max[...] + jnp.log(jnp.where(sums > 0.0, sums, 1.0))
-        slow = jnp.where(sums > 0.0, slow, NEG_FILL)
-        high = jnp.maximum(fast, slow)
-        part_ref[...] = high + jnp.log(jnp.exp(fast - high) + jnp.exp(slow - high))
-
-
-def second_kernel(
-    dev_count, pairs_ref, count_ref, src_ref, logw_ref, fs_ref, dual_ref, tab_ref,
-    pot_ref, map_ref, sum_ref,
-    kept, fs_col, acc,
-):
-    scale = LOG2E / math.sqrt(EMB)
-    rows = src_ref.shape[1]
-    myself = lax.axis_index("group") * dev_count + lax.axis_index("dev")
-    position_of = functools.partial(table_position, pairs_ref, dev_count, myself)
-    sum_ref[...] = jnp.zeros_like(sum_ref)
-    ones = jnp.ones((rows, LANES), jnp.bfloat16)
-
-    @pl.loop(0, BLK_DEV)
-    def _(blk):
-        count = count_ref[myself * BLK_DEV + blk]
-        first_source = fs_ref[blk]
-        fs_col[...] = as_columns(first_source * LOG2E)
-        acc[...] = jnp.zeros_like(acc)
-
-        def row_work(width):
-            for slot in range(width):
-                position = position_of(blk, slot)
-                dual = jnp.where(slot < count, dual_ref[position] * LOG2E, NEG_FILL)
-                points = tab_ref[position]
-                beside = jnp.concatenate([points, ones], axis=1)
-                for part in range(rows // LANES):
-                    span = pl.ds(part * LANES, LANES)
-                    shift = jnp.concatenate([fs_col[span, :]] * (rows // LANES), axis=1)
-                    plan = jnp.exp2(
-                        raw_scores(src_ref[blk, span, :], points) * scale + (dual + shift)
-                    ).astype(jnp.bfloat16)
-                    kept[slot, span, :] = plan
-                    acc[span, :] += jnp.dot(plan, beside, preferred_element_type=jnp.float32)
-
-        by_width(count, row_work)
-        row_col = acc[:, LANES:]
-        map_ref[blk] = acc[:, :LANES] / row_col
-        row_sum = as_row(row_col)
-        logw = logw_ref[blk]
-        pot_ref[blk] = logw + first_source - jnp.log(row_sum)
-        weights = weight_rows(jnp.exp(logw) / row_sum)
-
-        def column_work(width):
-            for slot in range(width):
-                here = column_sums(weights, kept, slot)
-                sum_ref[position_of(blk, slot)] += jnp.where(slot < count, here, 0.0)
-
-        by_width(count, column_work)
+                here = high + jnp.log(total)
+                old = part_ref[position]
+                new = jnp.maximum(old, here)
+                part_ref[position] = new + jnp.log(jnp.exp(old - new) + jnp.exp(here - new))
+
+        fs_ref[...] = logw_ref[...] - as_row(row_acc[...])
 
 
 def deliver_kernel(
@@ -480,8 +427,12 @@
 
     lax.fori_loop(1, dev_count, start(to_dev), 0)
     lax.fori_loop(1, group_count, start(to_group), 0)
-    lax.fori_loop(1, dev_count, wait(to_dev), 0)
-    lax.fori_loop(1, group_count, wait(to_group), 0)
+
+    def finish():
+        lax.fori_loop(1, dev_count, wait(to_dev), 0)
+        lax.fori_loop(1, group_count, wait(to_group), 0)
+
+    return finish
 
 
 def picks_of_peers(pick_ref, pairs_ref, dev_count, group_count, me_group, me_dev):
@@ -493,59 +444,107 @@
     ]
 
 
-def settle_kernel(
-    dev_count, group_count, pick_ref, pairs_ref, part_ref, logw_ref, dual_ref,
-    inbox, outbox, send_a, recv_a, send_b, recv_b,
+def finish_kernel(
+    dev_count, group_count, pick_ref, pairs_ref, count_ref, part_ref, tgt_logw_ref, src_ref,
+    src_logw_ref, fs_ref, tab_ref,
+    pot_ref, map_ref, tgt_pot_ref,
+    inbox, outbox, dual_ref, inbox2, outbox2, kept, fs_col, acc, wts, col_sum,
+    send_a, recv_a, send_b, recv_b, send_c, recv_c,
 ):
     me_group, me_dev = lax.axis_index("group"), lax.axis_index("dev")
-    blocks = BLK_DEV
+    myself = me_group * dev_count + me_dev
+    blocks, rows = BLK_DEV, src_ref.shape[1]
+    scale = LOG2E / math.sqrt(EMB)
+    position_of = functools.partial(table_position, pairs_ref, dev_count, myself)
+    place = (dev_count, group_count, me_dev, me_group)
+    greet(*place)
+    arrived = exchange(part_ref, blocks, inbox, 0, send_a, recv_a, *place)
     empty = jnp.full(inbox.shape[1:], NEG_FILL, jnp.float32)
-    greet(dev_count, group_count, me_dev, me_group)
-    inbox[me_dev] = empty
-    inbox[dev_count + me_group] = empty
+    for at in (me_dev, dev_count + me_group):
+        inbox[at] = empty
+        inbox2[at] = jnp.zeros_like(empty)
+        dual_ref[blocks + at] = jnp.zeros_like(empty)
     picks = picks_of_peers(pick_ref, pairs_ref, dev_count, group_count, me_group, me_dev)
-    exchange(
-        part_ref, blocks, inbox, 0, send_a, recv_a, dev_count, group_count, me_dev, me_group
-    )
-    duals = []
+    fs_col[...] = as_columns(fs_ref[...] * LOG2E)
+    arrived()
     for q in range(blocks):
         terms = [part_ref[q]] + [
             jnp.where(pick == q, inbox[e], NEG_FILL) for e, pick in enumerate(picks)
         ]
         high = functools.reduce(jnp.maximum, terms)
         total = sum(jnp.exp(term - high) for term in terms)
-        duals.append(logw_ref[q] - (high + jnp.log(total)))
-        dual_ref[q] = duals[q]
+        dual_ref[q] = tgt_logw_ref[q] - (high + jnp.log(total))
+    duals = [dual_ref[q] for q in range(blocks)]
     for e, pick in enumerate(picks):
         chosen = duals[0]
         for q in range(1, blocks):
             chosen = jnp.where(pick == q, duals[q], chosen)
         outbox[e] = chosen
-    dual_ref[blocks + me_dev] = jnp.zeros_like(empty)
-    dual_ref[blocks + dev_count + me_group] = jnp.zeros_like(empty)
-    exchange(
-        outbox, 0, dual_ref, blocks, send_b, recv_b, dev_count, group_count, me_dev, me_group
+    exchange(outbox, 0, dual_ref, blocks, send_b, recv_b, *place)()
+
+    ones = jnp.ones((rows, LANES), jnp.bfloat16)
+
+    @pl.loop(0, blocks)
+    def _(blk):
+        count = count_ref[myself * blocks + blk]
+        for slot in range(SLOTS):
+            position = position_of(blk, slot)
+            dual = jnp.where(slot < count, dual_ref[position] * LOG2E, NEG_FILL)
+            points = tab_ref[position]
+            beside = jnp.concatenate([points, ones], axis=1)
+            for part in range(rows // LANES):
+                span = pl.ds(part * LANES, LANES)
+                here = pl.ds(blk * rows + part * LANES, LANES)
+                shift = jnp.concatenate([fs_col[here, :]] * (rows // LANES), axis=1)
+                plan = jnp.exp2(
+                    raw_scores(src_ref[blk, span, :], points) * scale + (dual + shift)
+                ).astype(jnp.bfloat16)
+                kept[blk * SLOTS + slot, span, :] = plan
+                product = jnp.dot(plan, beside, preferred_element_type=jnp.float32)
+                acc[here, :] = product if slot == 0 else acc[here, :] + product
+
+    row_sum = as_row(acc[:, LANES:])
+    logw = src_logw_ref[...]
+    weights = weight_rows(jnp.exp(logw) / row_sum)
+    for blk in range(blocks):
+        wts[blk] = weights[:, blk * rows : (blk + 1) * rows]
+
+    @pl.loop(0, blocks)
+    def _(blk):
+        for slot in range(SLOTS):
+            col_sum[pl.ds(blk * SLOTS + slot, 1), :] = column_sums(
+                wts[blk], kept[blk * SLOTS + slot]
+            )
+
+    table, pairs = part_ref.shape[0], blocks * SLOTS
+    row_at = lax.broadcasted_iota(jnp.int32, (table, pairs), 0)
+    col_at = lax.broadcasted_iota(jnp.int32, (table, pairs), 1)
+    into = jnp.full((table, pairs), -1, jnp.int32)
+    for blk in range(blocks):
+        count = count_ref[myself * blocks + blk]
+        for slot in range(SLOTS):
+            position = jnp.where(slot < count, position_of(blk, slot), -1)
+            into = jnp.where(col_at == blk * SLOTS + slot, position, into)
+    gathered = lax.dot_general(
+        jnp.where(into == row_at, 1.0, 0.0),
+        col_sum[...],
+        (((1,), (0,)), ((), ())),
+        precision=lax.Precision.HIGHEST,
+        preferred_element_type=jnp.float32,
     )
-
-
-def close_kernel(
-    dev_count, group_count, pick_ref, pairs_ref, sum_ref, logw_ref, first_ref, pot_ref,
-    inbox, send_a, recv_a,
-):
-    me_group, me_dev = lax.axis_index("group"), lax.axis_index("dev")
-    blocks = BLK_DEV
-    greet(dev_count, group_count, me_dev, me_group)
-    inbox[me_dev] = jnp.zeros(inbox.shape[1:], jnp.float32)
-    inbox[dev_count + me_group] = jnp.zeros(inbox.shape[1:], jnp.float32)
-    picks = picks_of_peers(pick_ref, pairs_ref, dev_count, group_count, me_group, me_dev)
-    exchange(
-        sum_ref, blocks, inbox, 0, send_a, recv_a, dev_count, group_count, me_dev, me_group
-    )
+    for e in range(table):
+        outbox2[e] = gathered[e : e + 1]
+    arrived = exchange(outbox2, blocks, inbox2, 0, send_c, recv_c, *place)
+    pot_ref[...] = logw + fs_ref[...] - jnp.log(row_sum)
+    for blk in range(blocks):
+        span = pl.ds(blk * rows, rows)
+        map_ref[blk] = acc[span, :LANES] / acc[span, LANES:]
+    arrived()
     for q in range(blocks):
-        total = sum_ref[q]
+        total = outbox2[q]
         for e, pick in enumerate(picks):
-            total = total + jnp.where(pick == q, inbox[e], 0.0)
-        pot_ref[q] = logw_ref[q] - jnp.log(total) + first_ref[q]
+            total = total + jnp.where(pick == q, inbox2[e], 0.0)
+        tgt_pot_ref[q] = tgt_logw_ref[q] - jnp.log(total) + dual_ref[q]
 
 
 def shards(source_points, target_points, source_logw, target_logw, pair_targets, pair_count):
@@ -557,8 +556,8 @@
     peers = dev_count + group_count
     sources = source_points.reshape(blocks, rows, EMB)
     targets = target_points.reshape(blocks, rows, EMB)
-    log_src = source_logw.reshape(blocks, 1, rows)
-    log_tgt = target_logw.reshape(blocks, rows // LANES, LANES)
+    log_src = source_logw.reshape(1, blocks * rows)
+    log_tgt = target_logw.reshape(blocks, 1, rows)
 
     plane = dev_count * blocks
     named = pair_targets.T
@@ -573,7 +572,7 @@
     vmem = pl.BlockSpec(memory_space=pltpu.VMEM)
     anywhere = pl.BlockSpec(memory_space=pl.ANY)
     f32 = jnp.float32
-    kept = pltpu.VMEM((slots, rows, rows), jnp.bfloat16)
+    kept = pltpu.VMEM((blocks * slots, rows, rows), jnp.bfloat16)
     pairs = blocks * slots
     dma = pltpu.SemaphoreType.DMA
     block = (rows, EMB)
@@ -605,83 +604,60 @@
     first_source, part = pl.pallas_call(
         functools.partial(first_kernel, dev_count),
         out_shape=(
-            jax.ShapeDtypeStruct((blocks, 1, rows), f32),
+            jax.ShapeDtypeStruct((1, blocks * rows), f32),
             jax.ShapeDtypeStruct((table, 1, rows), f32),
         ),
         in_specs=[smem, smem, vmem, vmem, vmem],
         out_specs=(vmem, vmem),
         scratch_shapes=[
             kept,
+            pltpu.VMEM((blocks * rows, LANES), f32),
+            pltpu.VMEM((blocks, 16, rows), jnp.bfloat16),
+            pltpu.VMEM((1, rows), f32),
             pltpu.VMEM((rows, LANES), f32),
-            pltpu.VMEM((slots, 1, rows), f32),
-            pltpu.VMEM((table, 1, rows), f32),
-            pltpu.VMEM((table, 1, rows), f32),
             pltpu.VMEM((rows, LANES), f32),
-            pltpu.SMEM((1,), jnp.int32),
         ],
-        compiler_params=pltpu.CompilerParams(vmem_limit_bytes=VMEM_LIMIT),
+        compiler_params=pltpu.CompilerParams(vmem_limit_bytes=PAIR_LIMIT),
         cost_estimate=pl.CostEstimate(
             flops=4 * pairs * rows * rows * EMB, bytes_accessed=6 * 2**20, transcendentals=pairs * rows * rows
         ),
         name="first_pass",
     )(named, pair_count, sources, log_src, delivered)
 
-    small = (rows // LANES, LANES)
-    sems = pltpu.SemaphoreType.DMA((peers,))
-    dual = pl.pallas_call(
-        functools.partial(settle_kernel, dev_count, group_count),
-        out_shape=jax.ShapeDtypeStruct((table, *small), f32),
-        in_specs=[smem, smem, vmem, vmem],
-        out_specs=vmem,
-        scratch_shapes=[
-            pltpu.VMEM((peers, *small), f32),
-            pltpu.VMEM((peers, *small), f32),
-            sems,
-            sems,
-            sems,
-            sems,
-        ],
-        compiler_params=pltpu.CompilerParams(
-            collective_id=0, has_side_effects=True, vmem_limit_bytes=4 * 2**20
+    row = pltpu.VMEM((peers, 1, rows), f32)
+    full = pltpu.VMEM((table, 1, rows), f32)
+    potential, mapped, target_potential = pl.pallas_call(
+        functools.partial(finish_kernel, dev_count, group_count),
+        out_shape=(
+            jax.ShapeDtypeStruct((1, blocks * rows), f32),
+            jax.ShapeDtypeStruct((blocks, rows, EMB), f32),
+            jax.ShapeDtypeStruct((blocks, 1, rows), f32),
         ),
-        name="settle_first",
-    )(pick, named, part.reshape(table, *small), log_tgt)
-
-    potential, mapped, col_sums = pl.pallas_call(
-        functools.partial(second_kernel, dev_count),
-        out_shape=(
-            jax.ShapeDtypeStruct((blocks, 1, rows), f32),
-            jax.ShapeDtypeStruct((blocks, rows, EMB), f32),
-            jax.ShapeDtypeStruct((table, 1, rows), f32),
-        ),
-        in_specs=[smem, smem, vmem, vmem, vmem, vmem, vmem],
+        in_specs=[smem, smem, smem, vmem, vmem, vmem, vmem, vmem, vmem],
         out_specs=(vmem, vmem, vmem),
         scratch_shapes=[
+            row,
+            row,
+            full,
+            row,
+            full,
             kept,
-            pltpu.VMEM((rows, LANES), f32),
-            pltpu.VMEM((rows, 2 * LANES), f32),
-        ],
-        compiler_params=pltpu.CompilerParams(vmem_limit_bytes=VMEM_LIMIT),
+            pltpu.VMEM((blocks * rows, LANES), f32),
+            pltpu.VMEM((blocks * rows, 2 * LANES), f32),
+            pltpu.VMEM((blocks, 16, rows), jnp.bfloat16),
+            pltpu.VMEM((pairs, rows), f32),
+        ]
+        + [dma((peers,))] * 6,
+        compiler_params=pltpu.CompilerParams(
+            collective_id=0, has_side_effects=True, vmem_limit_bytes=PAIR_LIMIT
+        ),
         cost_estimate=pl.CostEstimate(
             flops=8 * pairs * rows * rows * EMB, bytes_accessed=7 * 2**20, transcendentals=pairs * rows * rows
         ),
-        name="second_pass",
+        name="finish",
     )(
-        named, pair_count, sources, log_src, first_source,
-        dual.reshape(table, 1, rows), delivered,
+        pick, named, pair_count, part, log_tgt, sources, log_src, first_source, delivered
     )
-
-    target_potential = pl.pallas_call(
-        functools.partial(close_kernel, dev_count, group_count),
-        out_shape=jax.ShapeDtypeStruct((blocks, *small), f32),
-        in_specs=[smem, smem, vmem, vmem, vmem],
-        out_specs=vmem,
-        scratch_shapes=[pltpu.VMEM((peers, *small), f32), sems, sems],
-        compiler_params=pltpu.CompilerParams(
-            collective_id=1, has_side_effects=True, vmem_limit_bytes=4 * 2**20
-        ),
-        name="settle_second",
-    )(pick, named, col_sums.reshape(table, *small), log_tgt, dual)
     return (
         potential.reshape(blocks * rows),
         target_potential.reshape(blocks * rows),

time: 113 us -> 117 us (1.035)
  Pallas kernels: 108 us -> 111 us
  local copies, waits for them, and re-layouts: 3.18 us -> 4.74 us
    pallas_call x3 -> x1, Pallas kernels: 58.5 us -> 61.7 us  [shards(): pl.pallas_call(functools.partial(finish_kernel, dev_count, group_count),...]
    unnamed x13 -> x17, local copies, waits for them, and re-layouts: 2.37 us -> 3.95 us
where the time goes in v4:
time: 117 us
  Pallas kernels  111 us (95%)
  local copies, waits for them, and re-layouts  4.74 us (4%)
    pallas_call x1, Pallas kernels, shards(): pl.pallas_call(functools.partial(finish_kernel, dev_count, group_count),...  61.7 us
    pallas_call x1, Pallas kernels, shards(): pl.pallas_call(functools.partial(deliver_kernel, dev_count, group_count),...  42 us
    pallas_call x1, Pallas kernels, shards(): pl.pallas_call(functools.partial(first_kernel, dev_count), out_shape=(jax...  6.8 us
    unnamed x17, local copies, waits for them, and re-layouts  3.95 us

profile of v4, /device:TPU:1, one launch (start us, length us, event | category | flops | bytes accessed | tf_op | source)
XLA Modules:
  0.0 116.7 jit_solution(1662947662152218391)
XLA Ops:
  0.6 0.0 copy-start.6
  0.6 0.0 copy-start.2
  0.7 0.0 copy-start.4
  0.7 0.8 dynamic_slice.6
  1.5 0.7 fusion.1
  2.2 0.0 copy-start
  2.2 1.0 copy-done
  3.2 0.0 copy-start.1
  3.2 0.7 copy-done.1
  3.9 0.0 copy-start.3
  3.9 42.0 %deliver_blocks.1.tab_ref = bf16[40,512,128]{2,1,0:T(8,128)(2,1)S(1)} custom-call(s32[32,128]{1,0:T(8,128)S(1)} %select_reduce_fusion.pick_ref, s32[8,512]{1,0:T(8,128)S(1)} %bitcast.16, bf16[4,512,128]{2,1,0:T(8,128)(2,1)S(1)} %bitcast.15), custom_call_target="tpu_custom_call" | custom-call | tf_op jit(solution)/shard_map/deliver_blocks/pallas_call | solution.py:580
  46.0 0.0 copy-done.6
  46.0 0.0 copy-done.2
  46.0 0.0 copy-done.4
  46.0 0.0 copy-done.3
  46.0 0.0 copy-start.5
  46.0 6.8 %first_pass.1 = (f32[1,2048]{1,0:T(1,128)S(1)}, f32[40,1,512]{2,1,0:T(1,128)S(1)}) custom-call(s32[8,512]{1,0:T(8,128)S(1)} %bitcast.17, s32[512]{0:T(512)S(1)} %copy-done.6, bf16[4,512,128]{2,1,0:T(8,128)(2,1)S(1)} %bitcast.21, f32[1,2048]{1,0:T(1,128)S(1)} %bitcast.23, bf16[40,512,128]{2,1,0:T(8,128)(2,1)S(1)} %deliver_blocks.1.tab_ref), custom_call_target="tpu_custom_call" | custom-call | flops 4294967296 | bytes 6291456 | tf_op jit(solution)/shard_map/first_pass/pallas_call | solution.py:604
  52.9 0.0 copy-done.5
  52.9 61.7 %finish.1 = (f32[1,2048]{1,0:T(1,128)S(1)}, f32[4,512,128]{2,1,0:T(8,128)S(1)}, f32[4,1,512]{2,1,0:T(1,128)S(1)}) custom-call(s32[32,128]{1,0:T(8,128)S(1)} %select_reduce_fusion.pick_ref, s32[8,512]{1,0:T(8,128)S(1)} %bitcast.18, s32[512]{0:T(512)S(1)} %copy-done.6, f32[40,1,512]{2,1,0:T(1,128)S(1)} %get-tuple-element.8.part_ref, ...), custom_call_target="tpu_custom_call" | custom-call | flops 8589934592 | bytes 7340032 | tf_op jit(solution)/shard_map/finish/pallas_call | solution.py:629
  114.6 0.6 copy.12
  115.2 0.6 copy.13
  115.8 1.0 copy.14
  (1 shorter events, 0.0 us)
Async XLA Ops:
  0.6 45.4 %copy-start.6 = (s32[512]{0:T(512)S(1)}, s32[512]{0:T(512)}, u32[]{:S(2)}) copy-start(s32[512]{0:T(512)} %count_ref.3) | copy-start | bytes 6148
  0.6 45.4 %copy-start.2 = (s32[512,8]{0,1:T(8,128)S(1)}, s32[512,8]{0,1:T(8,128)}, u32[]{:S(2)}) copy-start(s32[512,8]{0,1:T(8,128)} %param.10) | copy-start | bytes 49156
  0.7 45.4 %copy-start.4 = (f32[2048]{0:T(1024)S(1)}, f32[2048]{0:T(1024)}, u32[]{:S(2)}) copy-start(f32[2048]{0:T(1024)} %param.8) | copy-start | bytes 24580
  2.2 1.0 copy-start
  3.2 0.7 copy-start.1
  3.9 42.1 %copy-start.3 = (bf16[2048,128]{1,0:T(8,128)(2,1)S(1)}, bf16[2048,128]{1,0:T(8,128)(2,1)}, u32[]{:S(2)}) copy-start(bf16[2048,128]{1,0:T(8,128)(2,1)} %param.6) | copy-start | bytes 1572868
  46.0 6.8 %copy-start.5 = (f32[2048]{0:T(1024)S(1)}, f32[2048]{0:T(1024)}, u32[]{:S(2)}) copy-start(f32[2048]{0:T(1024)} %param.9) | copy-start | bytes 24580

commit v5 on v4

--- a/solution.py
+++ b/solution.py
@@ -18,7 +18,9 @@
 ROW_LOW, ROW_HIGH, COL_LOW = 1e-6, 1e30, 1e-22
 MESH = pl.DeviceIdType.MESH
 VMEM_LIMIT = 20 * 2**20
-PAIR_LIMIT = 36 * 2**20
+PAIR_LIMIT = 28 * 2**20
+FINISH_LIMIT = 52 * 2**20
+PREPARED = 3
 
 
 RING = 4
@@ -70,6 +72,13 @@
 
 def as_row(columns):
     return jnp.transpose(columns)[0:1]
+
+
+def lane_sums(columns):
+    high = columns.astype(jnp.bfloat16)
+    low = (columns - high.astype(jnp.float32)).astype(jnp.bfloat16)
+    parts = jnp.concatenate([high, low], axis=1)
+    return raw_scores(jnp.ones((16, parts.shape[1]), jnp.bfloat16), parts)[0:1]
 
 
 def weight_rows(weights):
@@ -128,13 +137,7 @@
 
         by_width(count, row_work)
 
-    row_sum = lax.dot_general(
-        jnp.ones((8, LANES), jnp.float32),
-        row_acc[...],
-        (((1,), (1,)), ((), ())),
-        precision=lax.Precision.HIGHEST,
-        preferred_element_type=jnp.float32,
-    )[0:1]
+    row_sum = lane_sums(row_acc[...])
     logw = logw_ref[...]
     fs_ref[...] = logw - jnp.log(row_sum)
     weights = weight_rows(jnp.exp(logw) / row_sum)
@@ -448,7 +451,7 @@
     dev_count, group_count, pick_ref, pairs_ref, count_ref, part_ref, tgt_logw_ref, src_ref,
     src_logw_ref, fs_ref, tab_ref,
     pot_ref, map_ref, tgt_pot_ref,
-    inbox, outbox, dual_ref, inbox2, outbox2, kept, fs_col, acc, wts, col_sum,
+    inbox, outbox, dual_ref, inbox2, outbox2, kept, ready, fs_col, acc, wts, col_sum,
     send_a, recv_a, send_b, recv_b, send_c, recv_c,
 ):
     me_group, me_dev = lax.axis_index("group"), lax.axis_index("dev")
@@ -466,6 +469,23 @@
         dual_ref[blocks + at] = jnp.zeros_like(empty)
     picks = picks_of_peers(pick_ref, pairs_ref, dev_count, group_count, me_group, me_dev)
     fs_col[...] = as_columns(fs_ref[...] * LOG2E)
+
+    def exponent(blk, part, points):
+        span = pl.ds(part * LANES, LANES)
+        shift = fs_col[pl.ds(blk * rows + part * LANES, LANES), :]
+        shift = jnp.concatenate([shift] * (rows // LANES), axis=1)
+        return raw_scores(src_ref[blk, span, :], points) * scale + shift
+
+    def prepare(first, last):
+        @pl.loop(first, last)
+        def _(blk):
+            for slot in range(SLOTS):
+                points = tab_ref[position_of(blk, slot)]
+                for part in range(rows // LANES):
+                    span = pl.ds(part * LANES, LANES)
+                    ready[blk * SLOTS + slot, span, :] = exponent(blk, part, points)
+
+    prepare(0, (PREPARED + 1) // 2)
     arrived()
     for q in range(blocks):
         terms = [part_ref[q]] + [
@@ -480,12 +500,12 @@
         for q in range(1, blocks):
             chosen = jnp.where(pick == q, duals[q], chosen)
         outbox[e] = chosen
-    exchange(outbox, 0, dual_ref, blocks, send_b, recv_b, *place)()
-
+    arrived = exchange(outbox, 0, dual_ref, blocks, send_b, recv_b, *place)
+    prepare((PREPARED + 1) // 2, PREPARED)
+    arrived()
     ones = jnp.ones((rows, LANES), jnp.bfloat16)
 
-    @pl.loop(0, blocks)
-    def _(blk):
+    def plans(blk, exponent_of):
         count = count_ref[myself * blocks + blk]
         for slot in range(SLOTS):
             position = position_of(blk, slot)
@@ -495,15 +515,24 @@
             for part in range(rows // LANES):
                 span = pl.ds(part * LANES, LANES)
                 here = pl.ds(blk * rows + part * LANES, LANES)
-                shift = jnp.concatenate([fs_col[here, :]] * (rows // LANES), axis=1)
-                plan = jnp.exp2(
-                    raw_scores(src_ref[blk, span, :], points) * scale + (dual + shift)
-                ).astype(jnp.bfloat16)
+                plan = jnp.exp2(exponent_of(slot, part, points) + dual).astype(jnp.bfloat16)
                 kept[blk * SLOTS + slot, span, :] = plan
                 product = jnp.dot(plan, beside, preferred_element_type=jnp.float32)
                 acc[here, :] = product if slot == 0 else acc[here, :] + product
 
-    row_sum = as_row(acc[:, LANES:])
+    @pl.loop(0, PREPARED)
+    def _(blk):
+        plans(
+            blk,
+            lambda slot, part, points: ready[
+                blk * SLOTS + slot, pl.ds(part * LANES, LANES), :
+            ],
+        )
+
+    for blk in range(PREPARED, blocks):
+        plans(blk, lambda slot, part, points: exponent(blk, part, points))
+
+    row_sum = lane_sums(acc[:, LANES:]) * (1.0 / LANES)
     logw = src_logw_ref[...]
     weights = weight_rows(jnp.exp(logw) / row_sum)
     for blk in range(blocks):
@@ -642,6 +671,7 @@
             row,
             full,
             kept,
+            pltpu.VMEM((PREPARED * slots, rows, rows), f32),
             pltpu.VMEM((blocks * rows, LANES), f32),
             pltpu.VMEM((blocks * rows, 2 * LANES), f32),
             pltpu.VMEM((blocks, 16, rows), jnp.bfloat16),
@@ -649,7 +679,7 @@
         ]
         + [dma((peers,))] * 6,
         compiler_params=pltpu.CompilerParams(
-            collective_id=0, has_side_effects=True, vmem_limit_bytes=PAIR_LIMIT
+            collective_id=0, has_side_effects=True, vmem_limit_bytes=FINISH_LIMIT
         ),
         cost_estimate=pl.CostEstimate(
             flops=8 * pairs * rows * rows * EMB, bytes_accessed=7 * 2**20, transcendentals=pairs * rows * rows

time: 117 us -> 115 us (0.983)
  Pallas kernels: 111 us -> 109 us
    pallas_call x1, Pallas kernels: 61.7 us -> 57.2 us  [shards(): pl.pallas_call(functools.partial(finish_kernel, dev_count, group_count),...]
    pallas_call x1, Pallas kernels: 6.8 us -> 9.54 us  [shards(): pl.pallas_call(functools.partial(first_kernel, dev_count), out_shape=(jax...]
    unnamed x17 -> x19, local copies, waits for them, and re-layouts: 3.95 us -> 3.95 us
where the time goes in v5:
time: 115 us
  Pallas kernels  109 us (95%)
  local copies, waits for them, and re-layouts  4.74 us (4%)
    pallas_call x1, Pallas kernels, shards(): pl.pallas_call(functools.partial(finish_kernel, dev_count, group_count),...  57.2 us
    pallas_call x1, Pallas kernels, shards(): pl.pallas_call(functools.partial(deliver_kernel, dev_count, group_count),...  42 us
    pallas_call x1, Pallas kernels, shards(): pl.pallas_call(functools.partial(first_kernel, dev_count), out_shape=(jax...  9.54 us
    unnamed x19, local copies, waits for them, and re-layouts  3.95 us

profile of v5, /device:TPU:1, one launch (start us, length us, event | category | flops | bytes accessed | tf_op | source)
XLA Modules:
  0.0 115.0 jit_solution(4241633957969113321)
XLA Ops:
  0.6 0.0 copy-start.7
  0.6 0.0 copy-start.3
  0.7 0.0 copy-start.5
  0.7 0.8 dynamic_slice.6
  1.5 0.7 fusion.1
  2.2 0.0 copy-start.1
  2.2 1.0 copy-done.1
  3.2 0.0 copy-start.2
  3.2 0.7 copy-done.2
  3.9 0.0 copy-start.4
  3.9 42.0 %deliver_blocks.1.tab_ref = bf16[40,512,128]{2,1,0:T(8,128)(2,1)S(1)} custom-call(s32[32,128]{1,0:T(8,128)S(1)} %select_reduce_fusion.pick_ref, s32[8,512]{1,0:T(8,128)S(1)} %bitcast.16, bf16[4,512,128]{2,1,0:T(8,128)(2,1)S(1)} %bitcast.15), custom_call_target="tpu_custom_call" | custom-call | tf_op jit(solution)/shard_map/deliver_blocks/pallas_call | solution.py:609
  46.0 0.0 copy-done.7
  46.0 0.0 copy-done.3
  46.0 0.0 copy-done.5
  46.0 0.0 copy-done.4
  46.0 0.0 copy-start
  46.0 0.0 copy-start.6
  46.1 9.5 %first_pass.1 = (f32[1,2048]{1,0:T(1,128)S(1)}, f32[40,1,512]{2,1,0:T(1,128)S(1)}) custom-call(s32[8,512]{1,0:T(8,128)S(1)} %bitcast.17, s32[512]{0:T(512)S(1)} %copy-done.7, bf16[4,512,128]{2,1,0:T(8,128)(2,1)S(1)} %bitcast.21, f32[1,2048]{1,0:T(1,128)S(1)} %bitcast.23, bf16[40,512,128]{2,1,0:T(8,128)(2,1)S(1)} %deliver_blocks.1.tab_ref), custom_call_target="tpu_custom_call" | custom-call | flops 4294967296 | bytes 6291456 | tf_op jit(solution)/shard_map/first_pass/pallas_call | solution.py:633
  55.6 0.0 copy-done
  55.6 0.0 copy-done.6
  55.6 57.2 %finish.1 = (f32[1,2048]{1,0:T(1,128)S(1)}, f32[4,512,128]{2,1,0:T(8,128)S(1)}, f32[4,1,512]{2,1,0:T(1,128)S(1)}) custom-call(s32[32,128]{1,0:T(8,128)S(1)} %select_reduce_fusion.pick_ref, s32[8,512]{1,0:T(8,128)S(1)} %bitcast.18, s32[512]{0:T(512)S(1)} %copy-done.7, f32[40,1,512]{2,1,0:T(1,128)S(1)} %get-tuple-element.8.part_ref, ...), custom_call_target="tpu_custom_call" | custom-call | flops 8589934592 | bytes 7340032 | tf_op jit(solution)/shard_map/finish/pallas_call | solution.py:658
  112.9 0.6 copy.12
  113.5 0.6 copy.13
  114.1 1.0 copy.14
  (1 shorter events, 0.0 us)
Async XLA Ops:
  0.6 45.4 %copy-start.7 = (s32[512]{0:T(512)S(1)}, s32[512]{0:T(512)}, u32[]{:S(2)}) copy-start(s32[512]{0:T(512)} %count_ref.3) | copy-start | bytes 6148
  0.6 45.4 %copy-start.3 = (s32[512,8]{0,1:T(8,128)S(1)}, s32[512,8]{0,1:T(8,128)}, u32[]{:S(2)}) copy-start(s32[512,8]{0,1:T(8,128)} %param.10) | copy-start | bytes 49156
  0.7 45.4 %copy-start.5 = (f32[2048]{0:T(1024)S(1)}, f32[2048]{0:T(1024)}, u32[]{:S(2)}) copy-start(f32[2048]{0:T(1024)} %param.8) | copy-start | bytes 24580
  2.2 1.0 copy-start.1
  3.2 0.7 copy-start.2
  3.9 42.1 %copy-start.4 = (bf16[2048,128]{1,0:T(8,128)(2,1)S(1)}, bf16[2048,128]{1,0:T(8,128)(2,1)}, u32[]{:S(2)}) copy-start(bf16[2048,128]{1,0:T(8,128)(2,1)} %param.6) | copy-start | bytes 1572868
  46.0 9.6 %copy-start = (bf16[40,512,128]{2,1,0:T(8,128)(2,1)}, bf16[40,512,128]{2,1,0:T(8,128)(2,1)S(1)}, u32[]{:S(2)}) copy-start(bf16[40,512,128]{2,1,0:T(8,128)(2,1)S(1)} %deliver_blocks.1.tab_ref) | copy-start | bytes 15728644
  46.0 9.6 %copy-start.6 = (f32[2048]{0:T(1024)S(1)}, f32[2048]{0:T(1024)}, u32[]{:S(2)}) copy-start(f32[2048]{0:T(1024)} %param.9) | copy-start | bytes 24580

commit v6 on v5

--- a/solution.py
+++ b/solution.py
@@ -28,11 +28,28 @@
 BRANCH = ((2, 0), (2, 1), (1, 0), (1, 1), (3, 0), (3, 1))
 
 
-def plane_picks(targets, counts, first, sources):
-    slots = lax.broadcasted_iota(jnp.int32, targets.shape, 0)
-    named = jnp.where(slots < counts[None, :], targets - first, -1)[:, None, :]
-    source = lax.broadcasted_iota(jnp.int32, (1, sources, 1), 1)
-    return jnp.max(jnp.where((named >> 2) == source, named & 3, -1), axis=0)
+def all_picks(pairs_ref, dev_count, group_count, me_group, me_dev):
+    plane = dev_count * BLK_DEV
+    first = me_group * plane
+    span = pl.ds(pl.multiple_of(first, plane), plane)
+    slots = lax.broadcasted_iota(jnp.int32, (SLOTS, plane), 0)
+    name, counts = pairs_ref[0:SLOTS, span], pairs_ref[SLOTS : SLOTS + 1, span]
+    named = jnp.where(slots < counts, name - first, -1)
+    source = lax.broadcasted_iota(jnp.int32, (dev_count, plane), 0)
+    picks = jnp.full((dev_count, plane), -1, jnp.int32)
+    for slot in range(SLOTS):
+        here = named[slot : slot + 1]
+        picks = jnp.maximum(picks, jnp.where((here >> 2) == source, here & 3, -1))
+    away = pairs_ref[1:2, :]
+    away = jnp.where((away >> 2) == me_group * dev_count + me_dev, away & 3, -1)
+    away = [away[:, g * plane : (g + 1) * plane] for g in range(group_count)]
+    bits = dev_count.bit_length() - 1
+    owner = name >> 2
+    there = jnp.where(
+        (owner >> bits) == me_group, owner & (dev_count - 1), dev_count + (owner >> bits)
+    )
+    places = jnp.where(owner == me_group * dev_count + me_dev, name & 3, BLK_DEV + there)
+    return picks, away, places, counts
 
 
 def pick_of_dev(pick_ref, taker, source):
@@ -42,24 +59,18 @@
     return first
 
 
-def pick_of_group(pairs_ref, dev_count, peer, me_group, me_dev):
-    base = (peer * dev_count + me_dev) * BLK_DEV
-    mine = me_group * dev_count + me_dev
-    found = jnp.int32(-1)
-    for row in range(BLK_DEV):
-        name = pairs_ref[1, base + row]
-        found = jnp.maximum(found, jnp.where(name // BLK_DEV == mine, name % BLK_DEV, -1))
-    return found
-
-
-def table_position(pairs_ref, dev_count, myself, blk, slot):
-    name = pairs_ref[slot, myself * BLK_DEV + blk]
-    owner = name // BLK_DEV
-    group = owner // dev_count
-    away = jnp.where(
-        group == myself // dev_count, owner % dev_count, dev_count + group
-    )
-    return jnp.where(owner == myself, name % BLK_DEV, BLK_DEV + away)
+def pick_of_group(pick_ref, dev_count, peer, me_dev):
+    return pick_of_dev(pick_ref, me_dev, dev_count + peer)
+
+
+def slot_reader(place_ref, me_dev):
+    def position_of(blk, slot):
+        return place_ref[slot, me_dev * BLK_DEV + blk]
+
+    def count_of(blk):
+        return place_ref[SLOTS, me_dev * BLK_DEV + blk]
+
+    return position_of, count_of
 
 
 def raw_scores(left, right):
@@ -109,19 +120,18 @@
 
 
 def first_kernel(
-    dev_count, pairs_ref, count_ref, src_ref, logw_ref, tab_ref,
+    place_ref, src_ref, logw_ref, tab_ref,
     fs_ref, part_ref,
     kept, row_acc, wts, fine_ref, col_max, col_total,
 ):
     factor = 1.0 / math.sqrt(EMB)
     scale = factor * LOG2E
     rows = src_ref.shape[1]
-    myself = lax.axis_index("group") * dev_count + lax.axis_index("dev")
-    position_of = functools.partial(table_position, pairs_ref, dev_count, myself)
+    position_of, count_of = slot_reader(place_ref, lax.axis_index("dev"))
 
     @pl.loop(0, BLK_DEV)
     def _(blk):
-        count = count_ref[myself * BLK_DEV + blk]
+        count = count_of(blk)
 
         def row_work(width):
             totals = jnp.zeros((rows, LANES), jnp.float32)
@@ -152,7 +162,7 @@
 
     @pl.loop(0, BLK_DEV)
     def _(blk):
-        count = count_ref[myself * BLK_DEV + blk]
+        count = count_of(blk)
 
         def column_work(width):
             fine = fine_ref[...]
@@ -175,7 +185,7 @@
 
         @pl.loop(0, BLK_DEV)
         def _(blk):
-            count = count_ref[myself * BLK_DEV + blk]
+            count = count_of(blk)
             col_max[...] = jnp.full_like(col_max, NEG_FILL)
             col_total[...] = jnp.zeros_like(col_total)
 
@@ -221,8 +231,9 @@
 
 
 def deliver_kernel(
-    dev_count, group_count, pick_ref, pairs_ref, tgt_ref, tab_ref,
-    prev_buf, next_buf, far_buf, relay_up, relay_down, stage,
+    dev_count, group_count, pairs_ref, tgt_hbm, src_hbm, src_logw_hbm,
+    tab_ref, pick_out, place_out, src_out, src_logw_out,
+    pick_ref, tgt_ref, prev_buf, next_buf, far_buf, relay_up, relay_down, stage,
     trunk_send, trunk_recv, stage_send, tab_recv, relay_recv, fwd_send, grp_recv, own_sem,
 ):
     me_group, me_dev = lax.axis_index("group"), lax.axis_index("dev")
@@ -245,6 +256,19 @@
             device_id_type=MESH,
         )
 
+    needs = [
+        pltpu.make_async_copy(src, dst, own_sem.at[n])
+        for n, (src, dst) in enumerate(
+            (
+                (tgt_hbm, tgt_ref),
+                (src_logw_hbm, src_logw_out),
+                (src_hbm, src_out),
+                (tgt_hbm, tab_ref.at[pl.ds(0, BLK_DEV)]),
+            )
+        )
+    ]
+    for copy in needs:
+        copy.start()
     barrier = pltpu.get_barrier_semaphore()
     near = [
         device(i, j, cc) for i, j in ((1, 0), (3, 0), (0, 1), (0, 3)) for cc in (0, 1)
@@ -258,6 +282,16 @@
             device_id=(lax.rem(me_group + step, group_count), me_dev),
             device_id_type=MESH,
         )
+    by_dev, by_group, places, counts = all_picks(
+        pairs_ref, dev_count, group_count, me_group, me_dev
+    )
+    place_out[0:SLOTS, :] = places
+    place_out[SLOTS : SLOTS + 1, :] = counts
+    pick_out[0:dev_count, :] = by_dev
+    for g, here in enumerate(by_group):
+        pick_out[dev_count + g : dev_count + g + 1, :] = here
+    known = pltpu.make_async_copy(pick_out, pick_ref, own_sem.at[len(needs)])
+    known.start()
     pl.semaphore_wait(barrier, len(near) + group_count - 1)
 
     low, top = pl.ds(0, half), pl.ds(half, half)
@@ -267,10 +301,10 @@
         return send(src.at[span], dst.at[span], trunk_send.at[n], trunk_recv.at[n], dev)
 
     trunks = [
-        trunk(0, tgt_ref, prev_buf, low, ahead),
-        trunk(1, tgt_ref, next_buf, top, behind),
-        trunk(2, tgt_ref, prev_buf, top, ahead),
-        trunk(3, tgt_ref, next_buf, low, behind),
+        trunk(0, tgt_hbm, prev_buf, low, ahead),
+        trunk(1, tgt_hbm, next_buf, top, behind),
+        trunk(2, tgt_hbm, prev_buf, top, ahead),
+        trunk(3, tgt_hbm, next_buf, low, behind),
         trunk(4, prev_buf, far_buf, low, ahead),
         trunk(5, next_buf, far_buf, top, behind),
     ]
@@ -324,14 +358,14 @@
             copy.start()
             sent.append(copy)
 
+    known.wait()
+    needs[0].wait()
     branch(0, tgt_ref)
-    own = pltpu.make_async_copy(tgt_ref, tab_ref.at[pl.ds(0, BLK_DEV)], own_sem.at[0])
-    own.start()
     from_groups = []
     for step in range(1, group_count):
         peer = lax.rem(me_group + step, group_count)
         at = RING * (len(BRANCH) + 1) + step - 1
-        pick = pick_of_group(pairs_ref, dev_count, peer, me_group, me_dev)
+        pick = pick_of_group(pick_ref, dev_count, peer, me_dev)
         stage[at] = tgt_ref[jnp.maximum(pick, 0)]
         copy = send(
             stage.at[at],
@@ -368,7 +402,8 @@
         ).wait_recv()
     for copy in from_groups:
         copy.wait_recv()
-    own.wait()
+    for copy in needs[1:]:
+        copy.wait()
 
 
 def greet(dev_count, group_count, me_dev, me_group):
@@ -438,27 +473,32 @@
     return finish
 
 
-def picks_of_peers(pick_ref, pairs_ref, dev_count, group_count, me_group, me_dev):
+def picks_of_peers(pick_ref, dev_count, group_count, me_group, me_dev):
     return [
         jnp.where(me_dev == e, -1, pick_of_dev(pick_ref, e, me_dev)) for e in range(dev_count)
     ] + [
-        jnp.where(me_group == e, -1, pick_of_group(pairs_ref, dev_count, e, me_group, me_dev))
+        jnp.where(me_group == e, -1, pick_of_group(pick_ref, dev_count, e, me_dev))
         for e in range(group_count)
     ]
 
 
 def finish_kernel(
-    dev_count, group_count, pick_ref, pairs_ref, count_ref, part_ref, tgt_logw_ref, src_ref,
-    src_logw_ref, fs_ref, tab_ref,
+    dev_count, group_count, pick_ref, place_ref, part_ref, tgt_logw_ref, src_hbm,
+    src_logw_ref, fs_ref, tab_hbm,
     pot_ref, map_ref, tgt_pot_ref,
-    inbox, outbox, dual_ref, inbox2, outbox2, kept, ready, fs_col, acc, wts, col_sum,
+    src_ref, tab_ref, own_sem, inbox, outbox, dual_ref, inbox2, outbox2, kept, ready, fs_col, acc, wts, col_sum,
     send_a, recv_a, send_b, recv_b, send_c, recv_c,
 ):
     me_group, me_dev = lax.axis_index("group"), lax.axis_index("dev")
-    myself = me_group * dev_count + me_dev
     blocks, rows = BLK_DEV, src_ref.shape[1]
+    needs = [
+        pltpu.make_async_copy(src_hbm, src_ref, own_sem.at[0]),
+        pltpu.make_async_copy(tab_hbm, tab_ref, own_sem.at[1]),
+    ]
+    for copy in needs:
+        copy.start()
     scale = LOG2E / math.sqrt(EMB)
-    position_of = functools.partial(table_position, pairs_ref, dev_count, myself)
+    position_of, count_of = slot_reader(place_ref, me_dev)
     place = (dev_count, group_count, me_dev, me_group)
     greet(*place)
     arrived = exchange(part_ref, blocks, inbox, 0, send_a, recv_a, *place)
@@ -467,7 +507,7 @@
         inbox[at] = empty
         inbox2[at] = jnp.zeros_like(empty)
         dual_ref[blocks + at] = jnp.zeros_like(empty)
-    picks = picks_of_peers(pick_ref, pairs_ref, dev_count, group_count, me_group, me_dev)
+    picks = picks_of_peers(pick_ref, dev_count, group_count, me_group, me_dev)
     fs_col[...] = as_columns(fs_ref[...] * LOG2E)
 
     def exponent(blk, part, points):
@@ -485,6 +525,8 @@
                     span = pl.ds(part * LANES, LANES)
                     ready[blk * SLOTS + slot, span, :] = exponent(blk, part, points)
 
+    for copy in needs:
+        copy.wait()
     prepare(0, (PREPARED + 1) // 2)
     arrived()
     for q in range(blocks):
@@ -506,7 +548,7 @@
     ones = jnp.ones((rows, LANES), jnp.bfloat16)
 
     def plans(blk, exponent_of):
-        count = count_ref[myself * blocks + blk]
+        count = count_of(blk)
         for slot in range(SLOTS):
             position = position_of(blk, slot)
             dual = jnp.where(slot < count, dual_ref[position] * LOG2E, NEG_FILL)
@@ -550,7 +592,7 @@
     col_at = lax.broadcasted_iota(jnp.int32, (table, pairs), 1)
     into = jnp.full((table, pairs), -1, jnp.int32)
     for blk in range(blocks):
-        count = count_ref[myself * blocks + blk]
+        count = count_of(blk)
         for slot in range(SLOTS):
             position = jnp.where(slot < count, position_of(blk, slot), -1)
             into = jnp.where(col_at == blk * SLOTS + slot, position, into)
@@ -579,7 +621,6 @@
 def shards(source_points, target_points, source_logw, target_logw, pair_targets, pair_count):
     group_count = lax.axis_size("group")
     dev_count = lax.axis_size("dev")
-    group_idx = lax.axis_index("group")
     blocks, rows, slots = BLK_DEV, BLOCK, SLOTS
     table = blocks + dev_count + group_count
     peers = dev_count + group_count
@@ -588,14 +629,7 @@
     log_src = source_logw.reshape(1, blocks * rows)
     log_tgt = target_logw.reshape(blocks, 1, rows)
 
-    plane = dev_count * blocks
-    named = pair_targets.T
-    pick = plane_picks(
-        lax.dynamic_slice_in_dim(named, group_idx * plane, plane, 1),
-        lax.dynamic_slice_in_dim(pair_count, group_idx * plane, plane, 0),
-        group_idx * plane,
-        dev_count,
-    )
+    named = jnp.concatenate([pair_targets.T, pair_count[None, :]], axis=0)
 
     smem = pl.BlockSpec(memory_space=pltpu.SMEM)
     vmem = pl.BlockSpec(memory_space=pltpu.VMEM)
@@ -606,12 +640,23 @@
     dma = pltpu.SemaphoreType.DMA
     block = (rows, EMB)
     lots = RING * (len(BRANCH) + 1) + group_count - 1 + RING - 1
-    delivered = pl.pallas_call(
+    picks = (peers, dev_count * blocks)
+    hbm = pl.BlockSpec(memory_space=pltpu.HBM)
+    delivered, pick, places, near_src, near_log_src = pl.pallas_call(
         functools.partial(deliver_kernel, dev_count, group_count),
-        out_shape=jax.ShapeDtypeStruct((table, *block), jnp.bfloat16),
-        in_specs=[smem, smem, vmem],
-        out_specs=anywhere,
-        scratch_shapes=[pltpu.VMEM((blocks, *block), jnp.bfloat16)] * 3
+        out_shape=(
+            jax.ShapeDtypeStruct((table, *block), jnp.bfloat16),
+            jax.ShapeDtypeStruct(picks, jnp.int32),
+            jax.ShapeDtypeStruct((2 * slots, dev_count * blocks), jnp.int32),
+            jax.ShapeDtypeStruct((blocks, *block), jnp.bfloat16),
+            jax.ShapeDtypeStruct((1, blocks * rows), f32),
+        ),
+        in_specs=[vmem, hbm, hbm, hbm],
+        out_specs=(anywhere, vmem, vmem, anywhere, anywhere),
+        scratch_shapes=[
+            pltpu.SMEM(picks, jnp.int32),
+        ]
+        + [pltpu.VMEM((blocks, *block), jnp.bfloat16)] * 4
         + [pltpu.VMEM((RING, *block), jnp.bfloat16)] * 2
         + [
             pltpu.VMEM((lots, *block), jnp.bfloat16),
@@ -622,21 +667,21 @@
             dma((2 * RING,)),
             dma((2 * RING,)),
             dma((group_count,)),
-            dma((1,)),
+            dma((5,)),
         ],
         compiler_params=pltpu.CompilerParams(
             collective_id=2, has_side_effects=True, vmem_limit_bytes=VMEM_LIMIT
         ),
         name="deliver_blocks",
-    )(pick, named, targets)
+    )(named, targets, sources, log_src)
 
     first_source, part = pl.pallas_call(
-        functools.partial(first_kernel, dev_count),
+        first_kernel,
         out_shape=(
             jax.ShapeDtypeStruct((1, blocks * rows), f32),
             jax.ShapeDtypeStruct((table, 1, rows), f32),
         ),
-        in_specs=[smem, smem, vmem, vmem, vmem],
+        in_specs=[smem, vmem, vmem, vmem],
         out_specs=(vmem, vmem),
         scratch_shapes=[
             kept,
@@ -651,7 +696,7 @@
             flops=4 * pairs * rows * rows * EMB, bytes_accessed=6 * 2**20, transcendentals=pairs * rows * rows
         ),
         name="first_pass",
-    )(named, pair_count, sources, log_src, delivered)
+    )(places, near_src, near_log_src, delivered)
 
     row = pltpu.VMEM((peers, 1, rows), f32)
     full = pltpu.VMEM((table, 1, rows), f32)
@@ -662,9 +707,12 @@
             jax.ShapeDtypeStruct((blocks, rows, EMB), f32),
             jax.ShapeDtypeStruct((blocks, 1, rows), f32),
         ),
-        in_specs=[smem, smem, smem, vmem, vmem, vmem, vmem, vmem, vmem],
+        in_specs=[smem, smem, vmem, vmem, hbm, vmem, vmem, hbm],
         out_specs=(vmem, vmem, vmem),
         scratch_shapes=[
+            pltpu.VMEM((blocks, *block), jnp.bfloat16),
+            pltpu.VMEM((table, *block), jnp.bfloat16),
+            dma((2,)),
             row,
             row,
             full,
@@ -686,7 +734,7 @@
         ),
         name="finish",
     )(
-        pick, named, pair_count, part, log_tgt, sources, log_src, first_source, delivered
+        pick, places, part, log_tgt, sources, near_log_src, first_source, delivered
     )
     return (
         potential.reshape(blocks * rows),

time: 115 us -> 112 us (0.974)
  Pallas kernels: 109 us -> 105 us
    pallas_call x1, Pallas kernels: 57.2 us -> 54.1 us  [shards(): pl.pallas_call(functools.partial(finish_kernel, dev_count, group_count),...]
    unnamed x19 -> x15, local copies, waits for them, and re-layouts: 3.95 us -> 4.96 us
where the time goes in v6:
time: 112 us; the launch traced here: 111 us
  Pallas kernels  105 us (94%)
  local copies, waits for them, and re-layouts  4.96 us (4%)
    pallas_call x1, Pallas kernels, shards(): pl.pallas_call(functools.partial(finish_kernel, dev_count, group_count),...  54.1 us
    pallas_call x1, Pallas kernels, shards(): pl.pallas_call(functools.partial(deliver_kernel, dev_count, group_count),...  41.1 us
    pallas_call x1, Pallas kernels, shards(): pl.pallas_call(first_kernel, out_shape=(jax.ShapeDtypeStruct((1, blocks *...  9.32 us
    unnamed x15, local copies, waits for them, and re-layouts  4.96 us

profile of v6, /device:TPU:1, one launch (start us, length us, event | category | flops | bytes accessed | tf_op | source)
XLA Modules:
  0.0 110.9 jit_solution(7144411794642993518)
XLA Ops:
  0.6 0.7 pad_add_fusion.pairs_ref
  1.4 0.0 copy-start
  1.4 1.0 copy-done
  2.4 0.0 copy-start.1
  2.4 1.0 copy-done.1
  3.5 0.0 copy-start.3
  3.5 0.7 copy-done.3
  4.2 41.1 %deliver_blocks.1 = (bf16[40,512,128]{2,1,0:T(8,128)(2,1)S(1)}, s32[36,128]{1,0:T(8,128)S(1)}, s32[16,128]{1,0:T(8,128)S(1)}, bf16[4,512,128]{2,1,0:T(8,128)(2,1)S(1)}, f32[1,2048]{1,0:T(1,128)S(1)}) custom-call(s32[9,512]{1,0:T(8,128)S(1)} %pad_add_fusion.pairs_ref, bf16[4,512,128]{2,1,0:T(8,128)(2,1)S(1)} %bitcast.10, bf16[4,512,128]{2,1,0:T(8,128)(2,1)S(1)} %bitcast.11, ...), custom_call_target="tpu_custom_call" | custom-call | tf_op jit(solution)/shard_map/deliver_blocks/pallas_call | solution.py:645
  45.3 0.0 copy-start.4
  45.3 0.0 copy-start.2
  45.3 0.0 copy-start.5
  45.3 9.3 %first_pass.1 = (f32[1,2048]{1,0:T(1,128)S(1)}, f32[40,1,512]{2,1,0:T(1,128)S(1)}) custom-call(s32[16,128]{1,0:T(8,128)S(1)} %get-tuple-element.14.place_ref, bf16[4,512,128]{2,1,0:T(8,128)(2,1)S(1)} %get-tuple-element.15.src_ref, f32[1,2048]{1,0:T(1,128)S(1)} %get-tuple-element.16.logw_ref.src_logw_ref, ...), custom_call_target="tpu_custom_call" | custom-call | flops 4294967296 | bytes 6291456 | tf_op jit(solution)/shard_map/first_pass/pallas_call | solution.py:678
  54.7 0.0 copy-done.4
  54.7 0.0 copy-done.2
  54.7 0.0 copy-done.5
  54.7 54.1 %finish.1 = (f32[1,2048]{1,0:T(1,128)S(1)}, f32[4,512,128]{2,1,0:T(8,128)S(1)}, f32[4,1,512]{2,1,0:T(1,128)S(1)}) custom-call(s32[36,128]{1,0:T(8,128)S(1)} %get-tuple-element.13.pick_ref, s32[16,128]{1,0:T(8,128)S(1)} %get-tuple-element.14.place_ref, f32[40,1,512]{2,1,0:T(1,128)S(1)} %get-tuple-element.18.part_ref, f32[4,1,512]{2,1,0:T(1,128)S(1)} %bitcast.16, ...), custom_call_target="tpu_custom_call" | custom-call | flops 8589934592 | bytes 7340032 | tf_op jit(solution)/shard_map/finish/pallas_call | solution.py:703
  108.8 0.6 copy.12
  109.4 0.6 copy.13
  110.0 1.0 copy.14
Async XLA Ops:
  1.4 1.0 copy-start
  2.4 1.0 copy-start.1
  3.5 0.7 copy-start.3
  45.3 9.4 %copy-start.4 = (bf16[40,512,128]{2,1,0:T(8,128)(2,1)}, bf16[40,512,128]{2,1,0:T(8,128)(2,1)S(1)}, u32[]{:S(2)}) copy-start(bf16[40,512,128]{2,1,0:T(8,128)(2,1)S(1)} %get-tuple-element.17.tab_ref.tab_hbm) | copy-start | bytes 15728644
  45.3 9.4 %copy-start.2 = (bf16[2048,128]{1,0:T(8,128)(2,1)S(1)}, bf16[2048,128]{1,0:T(8,128)(2,1)}, u32[]{:S(2)}) copy-start(bf16[2048,128]{1,0:T(8,128)(2,1)} %param.6) | copy-start | bytes 1572868
  45.3 9.4 %copy-start.5 = (f32[2048]{0:T(1024)S(1)}, f32[2048]{0:T(1024)}, u32[]{:S(2)}) copy-start(f32[2048]{0:T(1024)} %param.9) | copy-start | bytes 24580
